TPU v7x, 512 devices: a whole 4x4x16 slice. The times are simulated.
512 devices in a mesh: snap: 16 (over z), space: 32 (over x, y, core).
Axes of the slice: x: 4, y: 4, z: 16, core: 2. Of those that a mesh axis runs over, the one named last changes fastest.
Arguments:
- snapshots: bfloat16 [49152, 4096], P('space', 'snap'), may hold values from -6 to 6
- cell_volume: float32 [49152], P('space'), may hold values from 0.0004 to 32, as said below
- counts: int32 [32], P('space'), may hold values from 6 to 24, as said below
- rim_rows: int32 [32, 2], P('space'), may hold values from 0 to 23, as said below
- jac_cols: int32 [768, 8], P('space'), may hold values from 0 to 25, as said below
- jacobian: bfloat16 [49152, 512], P('space'), may hold values from -0.25 to 0.25
- omega: bfloat16 [2, 512, 256], replicated, may hold values from -0.25 to 0.25
Outputs:
- basis: bfloat16 [49152, 4096], P('space', 'snap')
- jac_basis: bfloat16 [49152, 4096], P('space', 'snap')
Inputs may be any that keep to these rules, and one draw needn't show every extreme that they name: `counts`: some partition has exactly 24 used blocks. `rim_rows`: the 2 entries of a partition are distinct blocks below its count; entry 1 is its last used block. `jac_cols`: entry 0 of each block row is the block's own index; every other entry is below the partition's count or at least 24. `cell_volume`: Positive.
All inputs are finite; a program needn't handle non-finite values.
Results may differ from a plain program's by a relative error of at most 0.011.
Values may be sent and summed in bfloat16 or wider, within the bound.
A program may use at most 64 MiB of HBM per device.

v0:
```python
import jax
import jax.numpy as jnp
from jax import lax
from jax.sharding import PartitionSpec as P

BLOCK = 64
NNZ = 8
H = 1
LEVELS = 2


HIGH = lax.Precision.HIGHEST


def shifted(block, axis, distance):
    devices = range(lax.axis_size(axis))
    route = [(i - distance, i) for i in devices if i - distance in devices]
    return lax.ppermute(block, axis, route)


def padded(array, sides, width):
    for axis, dim in sides:
        size, length = (lax.axis_size(axis), array.shape[dim])
        up = [(i, (i + 1) % size) for i in range(size - 1)]
        down = [(j, i) for i, j in up]
        last = lax.slice_in_dim(array, length - width, length, axis=dim)
        leading = lax.slice_in_dim(array, 0, width, axis=dim)
        before = lax.ppermute(last, axis, up)
        after = lax.ppermute(leading, axis, down)
        array = jnp.concatenate([before, array, after], axis=dim)
    return array


def inverse_factor(gram):
    factor = jnp.linalg.cholesky(gram)
    ident = jnp.eye(gram.shape[0], dtype=gram.dtype)
    return lax.linalg.triangular_solve(factor, ident, left_side=True, lower=True)


def merge_pair(lower, higher, mixing, weight):
    joined = jnp.concatenate([lower, higher], 1)
    sketch = jnp.dot(joined, mixing, preferred_element_type=jnp.float32)
    wide = joined.astype(jnp.float32)
    gram = jnp.dot((wide * weight[:, None]).T, wide, precision=HIGH)
    gram = lax.psum(gram, "space")
    mixed = mixing.astype(jnp.float32)
    reduced = jnp.dot(mixed.T, jnp.dot(gram, mixed, precision=HIGH), precision=HIGH)
    return jnp.dot(sketch, inverse_factor(reduced).T, precision=HIGH).astype(jnp.bfloat16)


def on_device(snapshots, cell_volume, counts, rim_rows, jac_cols, jacobian, omega):
    rows, rank = snapshots.shape
    blocks = rows // BLOCK
    total = rows * lax.axis_size("space")
    block_index = lax.broadcasted_iota(jnp.int32, (blocks, BLOCK), 0).reshape(rows)
    valid = (block_index < counts[0]).astype(jnp.float32)
    weight = cell_volume * valid / total
    local = snapshots.astype(jnp.float32) * valid[:, None]
    gram = jnp.dot((local * weight[:, None]).T, local, precision=HIGH)
    gram = lax.psum(gram, "space")
    current = jnp.dot(local, inverse_factor(gram).T, precision=HIGH).astype(jnp.bfloat16)
    position = lax.axis_index("snap")
    for level in range(LEVELS):
        step = 1 << level
        incoming = shifted(current, "snap", -step)
        current = merge_pair(current, incoming, omega[level], weight)
    for level in reversed(range(LEVELS)):
        step = 1 << level
        arriving = shifted(current, "snap", step)
        current = jnp.where(position // step % 2 == 1, arriving, current)
    blocked = current.reshape(blocks, BLOCK, rank)
    rims = jnp.take(blocked, rim_rows[0], axis=0).reshape(2 * H * BLOCK, rank)
    widened = padded(rims, (("space", 0),), H * BLOCK)
    outer = jnp.concatenate([widened[: H * BLOCK], widened[-H * BLOCK :]], 0).reshape(
        2 * H, BLOCK, rank
    )
    extended = jnp.concatenate([blocked, outer], 0)
    picked = jnp.take(extended, jac_cols, axis=0)
    matrix = jacobian.reshape(blocks, BLOCK, NNZ, BLOCK)
    product = jnp.einsum("bikj,bkjr->bir", matrix, picked, preferred_element_type=jnp.float32)
    product = product.reshape(rows, rank) * valid[:, None]
    return (current, product.astype(jnp.bfloat16))


def solution(mesh):
    in_specs = (
        P("space", "snap"),
        P("space"),
        P("space"),
        P("space", None),
        P("space", None),
        P("space", None),
        P(),
    )
    out_specs = (P("space", "snap"), P("space", "snap"))
    return jax.shard_map(
        on_device, mesh=mesh, in_specs=in_specs, out_specs=out_specs, check_vma=False
    )
```

profile of v0, /device:TPU:98, one launch (start us, length us, event | category | flops | bytes accessed | tf_op | source)
XLA Modules:
  0.0 780.0 jit_solution(10043081009032569571)
XLA Ops:
  14.3 134.8 %all-reduce.5.cloned.1.call-done = f32[256,256]{0,1:T(8,128)} async-done(((f32[256,256]{0,1:T(8,128)}), f32[256,256]{0,1:T(8,128)}) %all-reduce.5.cloned.1.call-update) | async-done | bytes 262160 | tf_op jit(solution)/shard_map/psum | solution.py:60
  151.2 11.7 %cholesky.172 = f32[128,128]{1,0:T(8,128)S(1)} custom-call(f32[128,128]{1,0:T(8,128)S(1)} %cholesky.270), custom_call_target="Cholesky" | custom-call | tf_op jit(solution)/shard_map/jit(cholesky)/cholesky | solution.py:35
  163.0 9.8 %custom-call.15 = f32[1,128,128]{1,2,0:T(8,128)S(1)} custom-call(f32[1,128,128]{2,1,0:T(8,128)S(1)} %get-tuple-element.70), custom_call_target="InvertDiagBlocksLowerTriangular" | custom-call | tf_op jit(solution)/shard_map/jit(cholesky)/cholesky | solution.py:35
  173.3 11.7 %cholesky.189 = f32[128,128]{1,0:T(8,128)S(1)} custom-call(f32[128,128]{1,0:T(8,128)S(1)} %convolution_subtract_fusion.5), custom_call_target="Cholesky" | custom-call | tf_op jit(solution)/shard_map/jit(cholesky)/cholesky | solution.py:35
  191.6 19.7 %custom-call.16 = f32[2,128,128]{1,2,0:T(8,128)S(1)} custom-call(f32[2,128,128]{2,1,0:T(8,128)S(1)} %get-tuple-element.24), custom_call_target="InvertDiagBlocksLowerTriangular" | custom-call | tf_op jit(solution)/shard_map/triangular_solve/custom-call.0 | solution.py:37
  216.4 20.3 %collective-permute-done = bf16[1536,256]{0,1:T(8,128)(2,1)S(1)} collective-permute-done((bf16[1536,256]{0,1:T(8,128)(2,1)S(1)}, bf16[1536,256]{0,1:T(8,128)(2,1)S(1)}, u32[]{:S(2)}, u32[]{:S(2)}) %collective-permute-start) | collective-permute-done | bytes 786464 | tf_op jit(solution)/shard_map/ppermute | solution.py:18
  242.6 131.8 %all-reduce.7.cloned.1.call-done = f32[512,512]{1,0:T(8,128)} async-done(((f32[512,512]{1,0:T(8,128)}), f32[512,512]{1,0:T(8,128)}) %all-reduce.7.cloned.1.call-update) | async-done | bytes 1048592 | tf_op jit(solution)/shard_map/psum | solution.py:45
  377.1 11.7 %cholesky.206 = f32[128,128]{1,0:T(8,128)S(1)} custom-call(f32[128,128]{1,0:T(8,128)S(1)} %cholesky.273), custom_call_target="Cholesky" | custom-call | tf_op jit(solution)/shard_map/jit(cholesky)/cholesky | solution.py:35
  389.5 9.8 %custom-call.17 = f32[1,128,128]{1,2,0:T(8,128)S(1)} custom-call(f32[1,128,128]{2,1,0:T(8,128)S(1)} %get-tuple-element.66), custom_call_target="InvertDiagBlocksLowerTriangular" | custom-call | tf_op jit(solution)/shard_map/jit(cholesky)/cholesky | solution.py:35
  399.8 11.7 %cholesky.223 = f32[128,128]{1,0:T(8,128)S(1)} custom-call(f32[128,128]{1,0:T(8,128)S(1)} %convolution_subtract_fusion.4), custom_call_target="Cholesky" | custom-call | tf_op jit(solution)/shard_map/jit(cholesky)/cholesky | solution.py:35
  417.9 19.7 %custom-call.18 = f32[2,128,128]{1,2,0:T(8,128)S(1)} custom-call(f32[2,128,128]{2,1,0:T(8,128)S(1)} %get-tuple-element.25), custom_call_target="InvertDiagBlocksLowerTriangular" | custom-call | tf_op jit(solution)/shard_map/triangular_solve/custom-call.0 | solution.py:37
  442.4 23.7 %collective-permute-done.1 = bf16[1536,256]{0,1:T(8,128)(2,1)S(1)} collective-permute-done((bf16[1536,256]{0,1:T(8,128)(2,1)S(1)}, bf16[1536,256]{0,1:T(8,128)(2,1)S(1)}, u32[]{:S(2)}, u32[]{:S(2)}) %collective-permute-start.1) | collective-permute-done | bytes 786464 | tf_op jit(solution)/shard_map/ppermute | solution.py:18
  471.5 146.8 %all-reduce.9.cloned.1.call-done = f32[512,512]{1,0:T(8,128)} async-done(((f32[512,512]{1,0:T(8,128)}), f32[512,512]{1,0:T(8,128)}) %all-reduce.9.cloned.1.call-update) | async-done | bytes 1048592 | tf_op jit(solution)/shard_map/psum | solution.py:45
  621.0 11.7 %cholesky.240 = f32[128,128]{1,0:T(8,128)S(1)} custom-call(f32[128,128]{1,0:T(8,128)S(1)} %cholesky.276), custom_call_target="Cholesky" | custom-call | tf_op jit(solution)/shard_map/jit(cholesky)/cholesky | solution.py:35
  633.3 9.8 %custom-call.19 = f32[1,128,128]{1,2,0:T(8,128)S(1)} custom-call(f32[1,128,128]{2,1,0:T(8,128)S(1)} %get-tuple-element.62), custom_call_target="InvertDiagBlocksLowerTriangular" | custom-call | tf_op jit(solution)/shard_map/jit(cholesky)/cholesky | solution.py:35
  643.7 11.9 %cholesky.257 = f32[128,128]{1,0:T(8,128)S(1)} custom-call(f32[128,128]{1,0:T(8,128)S(1)} %convolution_subtract_fusion.3), custom_call_target="Cholesky" | custom-call | tf_op jit(solution)/shard_map/jit(cholesky)/cholesky | solution.py:35
  661.8 19.7 %custom-call.20 = f32[2,128,128]{1,2,0:T(8,128)S(1)} custom-call(f32[2,128,128]{2,1,0:T(8,128)S(1)} %get-tuple-element.26), custom_call_target="InvertDiagBlocksLowerTriangular" | custom-call | tf_op jit(solution)/shard_map/triangular_solve/custom-call.0 | solution.py:37
  683.9 5.7 collective-permute-start.2
  689.6 33.5 %collective-permute-done.2 = bf16[1536,256]{1,0:T(8,128)(2,1)S(1)} collective-permute-done((bf16[1536,256]{1,0:T(8,128)(2,1)S(1)}, bf16[1536,256]{1,0:T(8,128)(2,1)S(1)}, u32[]{:S(2)}, u32[]{:S(2)}) %collective-permute-start.2) | collective-permute-done | bytes 786464 | tf_op jit(solution)/shard_map/ppermute | solution.py:18
  723.2 6.0 collective-permute-start.3
  729.5 15.9 %collective-permute-done.3 = bf16[1536,256]{1,0:T(8,128)(2,1)} collective-permute-done((bf16[1536,256]{1,0:T(8,128)(2,1)S(1)}, bf16[1536,256]{1,0:T(8,128)(2,1)}, u32[]{:S(2)}, u32[]{:S(2)}) %collective-permute-start.3) | collective-permute-done | bytes 786464 | tf_op jit(solution)/shard_map/ppermute | solution.py:18
  749.2 6.0 collective-permute-start.5
  758.5 8.0 %gather_fusion.1 = bf16[192,64,256]{2,1,0:T(8,128)(2,1)} fusion(bf16[26,64,256]{2,1,0:T(8,128)(2,1)S(1)} %pad_maximum_fusion.6, s32[1024]{0:T(1024)S(1)} %pad_clamp_fusion), kind=kCustom, calls=%fused_computation.1 | custom fusion | bytes 12583680 | tf_op jit(solution)/shard_map/jit(_take)/gather | solution.py:78
  766.5 5.5 fusion
  (129 shorter events, 75.7 us)
Async XLA Ops:
  7.2 142.0 %all-reduce.5.cloned.1.call-start = ((), (), s32[]{:S(2)}) async-start(), calls=%async_computation | async-start | bytes 524288 | tf_op jit(solution)/shard_map/psum | solution.py:60
  14.1 360.4 %all-reduce.7.cloned.1.call-start = ((), (), s32[]{:S(2)}) async-start(), calls=%async_computation.1 | async-start | bytes 2097152 | tf_op jit(solution)/shard_map/psum | solution.py:45
  173.0 39.1 %copy-start.3 = (bf16[1536,256]{1,0:T(8,128)(2,1)S(1)}, bf16[1536,256]{1,0:T(8,128)(2,1)}, u32[]{:S(2)}) copy-start(bf16[1536,256]{1,0:T(8,128)(2,1)} %param.10) | copy-start | bytes 2359300
  213.9 27.0 %copy-start.1 = (bf16[2,512,256]{2,1,0:T(8,128)(2,1)S(1)}, bf16[2,512,256]{2,1,0:T(8,128)(2,1)}, u32[]{:S(2)}) copy-start(bf16[2,512,256]{2,1,0:T(8,128)(2,1)} %param.16) | copy-start | bytes 1572868
  213.9 22.8 %collective-permute-start = (bf16[1536,256]{0,1:T(8,128)(2,1)S(1)}, bf16[1536,256]{0,1:T(8,128)(2,1)S(1)}, u32[]{:S(2)}, u32[]{:S(2)}) collective-permute-start(bf16[1536,256]{0,1:T(8,128)(2,1)S(1)} %convolution_convert_fusion.2), channel_id=1, source_target_pairs={{32,0},{64,32},{96,64},{128,96},{160,128},{192,160},{224,192},{256... | collective-permute-start | bytes 2359304 | tf_op jit(solution)/shard_map/ppermute | solution.py:18
  236.7 3.7 copy-start.5
  240.4 377.9 %all-reduce.9.cloned.1.call-start = ((), (), s32[]{:S(2)}) async-start(), calls=%async_computation.2 | async-start | bytes 2097152 | tf_op jit(solution)/shard_map/psum | solution.py:45
  440.1 26.0 %collective-permute-start.1 = (bf16[1536,256]{0,1:T(8,128)(2,1)S(1)}, bf16[1536,256]{0,1:T(8,128)(2,1)S(1)}, u32[]{:S(2)}, u32[]{:S(2)}) collective-permute-start(bf16[1536,256]{0,1:T(8,128)(2,1)S(1)} %convolution_convert_fusion.1), channel_id=1, source_target_pairs={{64,0},{96,32},{128,64},{160,96},{192,128},{224,160},{256,192},{28... | collective-permute-start | bytes 2359304 | tf_op jit(solution)/shard_map/ppermute | solution.py:18
  466.0 3.7 copy-start.6
  683.9 45.4 %copy-start.4 = (s32[24,8]{0,1:T(8,128)S(1)}, s32[24,8]{0,1:T(8,128)}, u32[]{:S(2)}) copy-start(s32[24,8]{0,1:T(8,128)} %param.14) | copy-start | bytes 2308
  683.9 45.6 %copy-start.7 = (s32[1,2]{1,0:T(1,128)S(1)}, s32[1,2]{1,0:T(1,128)}, u32[]{:S(2)}) copy-start(s32[1,2]{1,0:T(1,128)} %param.13) | copy-start | bytes 28
  683.9 39.2 %collective-permute-start.2 = (bf16[1536,256]{1,0:T(8,128)(2,1)S(1)}, bf16[1536,256]{1,0:T(8,128)(2,1)S(1)}, u32[]{:S(2)}, u32[]{:S(2)}) collective-permute-start(bf16[1536,256]{1,0:T(8,128)(2,1)S(1)} %convolution_convert_fusion), channel_id=1, source_target_pairs={{0,64},{32,96},{64,128},{96,160},{128,192},{160,224},{192,256},{22... | collective-permute-start | bytes 2359304 | tf_op jit(solution)/shard_map/ppermute | solution.py:18
  723.2 32.1 %copy-start.2 = (bf16[1536,512]{1,0:T(8,128)(2,1)S(1)}, bf16[1536,512]{1,0:T(8,128)(2,1)}, u32[]{:S(2)}) copy-start(bf16[1536,512]{1,0:T(8,128)(2,1)} %param.15) | copy-start | bytes 4718596
  723.2 22.2 %collective-permute-start.3 = (bf16[1536,256]{1,0:T(8,128)(2,1)S(1)}, bf16[1536,256]{1,0:T(8,128)(2,1)}, u32[]{:S(2)}, u32[]{:S(2)}) collective-permute-start(bf16[1536,256]{1,0:T(8,128)(2,1)S(1)} %broadcast_select_fusion), channel_id=1, source_target_pairs={{0,32},{32,64},{64,96},{96,128},{128,160},{160,192},{192,224},{224... | collective-permute-start | bytes 2359304 | tf_op jit(solution)/shard_map/ppermute | solution.py:18
  746.6 11.8 %copy-start = (bf16[1536,256]{1,0:T(8,128)(2,1)}, bf16[1536,256]{1,0:T(8,128)(2,1)S(1)}, u32[]{:S(2)}) copy-start(bf16[1536,256]{1,0:T(8,128)(2,1)S(1)} %broadcast_select_fusion.1) | copy-start | bytes 2359300
  747.3 11.1 %collective-permute-start.4 = (bf16[64,256]{1,0:T(8,128)(2,1)S(1)}, bf16[64,256]{1,0:T(8,128)(2,1)S(1)}, u32[]{:S(2)}, u32[]{:S(2)}) collective-permute-start(bf16[64,256]{1,0:T(8,128)(2,1)S(1)} %get-tuple-element.57), channel_id=1, source_target_pairs={{0,1},{1,2},{2,3},{3,4},{4,5},{5,6},{6,7},{7,8},{8,9},{9,10},{10,1... | collective-permute-start | bytes 98312 | tf_op jit(solution)/shard_map/ppermute | solution.py:28
  749.2 9.2 %collective-permute-start.5 = (bf16[64,256]{1,0:T(8,128)(2,1)S(1)}, bf16[64,256]{1,0:T(8,128)(2,1)S(1)}, u32[]{:S(2)}, u32[]{:S(2)}) collective-permute-start(bf16[64,256]{1,0:T(8,128)(2,1)S(1)} %get-tuple-element.58), channel_id=1, source_target_pairs={{1,0},{2,1},{3,2},{4,3},{5,4},{6,5},{7,6},{8,7},{9,8},{10,9},{11,1... | collective-permute-start | bytes 98312 | tf_op jit(solution)/shard_map/ppermute | solution.py:29
Sparse Core Ops, SparseCore 0:
  14.2 134.8 all-reduce.4
  240.5 133.8 all-reduce.6
  469.9 148.3 all-reduce.8
where the time goes:
time: 784 us; the launch traced here: 780 us
  waiting for transfers between devices  507 us (65%)
  other arithmetic  167 us (21%)
  matrix products  35.3 us (5%)
  local copies, waits for them, and re-layouts  25.7 us (3%)
  starting transfers between devices  25.1 us (3%)
  between operations  19.5 us (2%)
    psum x2, waiting for transfers between devices, merge_pair(): gram = lax.psum(gram, 'space')  279 us
    psum x1, waiting for transfers between devices, on_device(): gram = lax.psum(gram, 'space')  135 us
    another operation x20, other arithmetic, inverse_factor(): factor = jnp.linalg.cholesky(gram)  104 us
    ppermute x4, waiting for transfers between devices, shifted(): return lax.ppermute(block, axis, route)  93.4 us
    another operation x7, other arithmetic, inverse_factor(): lax.linalg.triangular_solve(factor, ident, left_side=True, lower=True)  59.1 us
    ppermute x4, starting transfers between devices, shifted(): return lax.ppermute(block, axis, route)  16.5 us
  transfers between devices with their start and end apart: 9, of which 7 were waited for; matrix products, arithmetic and copies ran while one was open for 1% of the time, Pallas kernels for 0%

commit v1 on v0

v1 whole, which is shorter than its diff:
```python
import functools

import jax
import jax.numpy as jnp
from jax import lax
from jax.experimental import pallas as pl
from jax.experimental.pallas import tpu as pltpu
from jax.sharding import PartitionSpec as P

BLOCK = 64
NNZ = 8
LEVELS = 2
F32, BF16 = jnp.float32, jnp.bfloat16
NN = ((1,), (0,))
NT = ((1,), (1,))
TN = ((0,), (0,))
MESH = pl.DeviceIdType.MESH
VMEM_LIMIT = 48 * 1024 * 1024


def split(a):
    hi = a.astype(BF16)
    return hi, (a - hi.astype(F32)).astype(BF16)

def mm(a, b, dims=((1,), (0,))):
    return lax.dot_general(a, b, (dims, ((), ())), preferred_element_type=F32)


def mm3(a, b, dims=NN):
    ah, al = split(a)
    bh, bl = split(b)
    return mm(ah, bh, dims) + (mm(ah, bl, dims) + mm(al, bh, dims))

def leaf(aq, W=32):
    T = W // 8
    def panel(k, _):
        r0 = pl.multiple_of(k * W, W)
        rows = aq[pl.ds(r0, W), :]
        diag = pltpu.roll(rows[:, :128], lax.rem(128 - r0, 128), axis=1)
        C = [[jnp.broadcast_to(diag[8*t:8*t+8, m:m+1], (8, 128)) for t in range(T)] for m in range(W)]
        lane = lax.broadcasted_iota(jnp.int32, (8, 128), 1)
        sub = lax.broadcasted_iota(jnp.int32, (8, 128), 0)
        E = [(lane == sub + 8*t).astype(F32) for t in range(T)]
        scale = [jnp.zeros((8, 128), F32) for t in range(T)]
        for j in range(W):
            tj, sj = divmod(j, 8)
            piv = jnp.broadcast_to(C[j][tj][sj:sj+1, :], (8, 128))
            r = pl.reciprocal(piv, approx=True)
            r = r * (2.0 - piv * r)
            f = [None]*T
            for t in range(tj, T):
                f[t] = C[j][t] * r
            f[tj] = jnp.where(sub > sj, f[tj], 0.0)
            for m in range(j + 1, W):
                tm, sm = divmod(m, 8)
                c = jnp.broadcast_to(C[j][tm][sm:sm+1, :], (8, 128))
                for t in range(tm, T):
                    C[m][t] = C[m][t] - f[t] * c
            e = jnp.broadcast_to(E[tj][sj:sj+1, :], (8, 128))
            for t in range(tj, T):
                E[t] = E[t] - f[t] * e
            scale[tj] = jnp.where(sub == sj, piv, scale[tj])
        E = [E[t] * lax.rsqrt(scale[t]) for t in range(T)]
        inv = jnp.concatenate(E, 0)[:, :W]
        R = mm3(inv, rows)
        low = jnp.transpose(R[:, :128])
        low = jnp.where(lax.broadcasted_iota(jnp.int32, low.shape, 0) >= r0 + W, low, 0.0)
        aq[...] = aq[...] - mm3(low, R)
        aq[pl.ds(r0, W), :] = R
        return 0
    lax.fori_loop(0, 128 // W, panel, 0)

def chol_inv(a, z, aq, W=32):
    eye = (lax.broadcasted_iota(jnp.int32, (128, 128), 0) == lax.broadcasted_iota(jnp.int32, (128, 128), 1)).astype(F32)
    aq[:, 128:] = eye
    aq[:, :128] = a[:128, :128]
    leaf(aq, W)
    z11 = aq[:, 128:]
    z[:128, :128] = z11
    l21 = mm3(a[128:, :128], z11, NT)
    aq[:, :128] = a[128:, 128:] - mm3(l21, l21, NT)
    aq[:, 128:] = eye
    m21 = mm3(l21, z11)
    leaf(aq, W)
    z22 = aq[:, 128:]
    z[128:, 128:] = z22
    z[128:, :128] = -mm3(z22, m21)
    z[:128, 128:] = jnp.zeros((128, 128), F32)


def reduce_gram(a_ref, b_ref, w_ref, out_ref, part, arrived, total, gathered, sems):
    n = part.shape[0]
    me = lax.axis_index("space")
    barrier = pltpu.get_barrier_semaphore()

    def greet(t, _):
        peer = lax.rem(me + t, n)
        pl.semaphore_signal(barrier, inc=1, device_id={"space": peer}, device_id_type=MESH)
        return 0

    lax.fori_loop(1, n, greet, 0)
    weighted = jnp.transpose(a_ref[...]).astype(F32) * w_ref[...]
    high, low = split(weighted)
    gram = mm(high, b_ref[...]) + mm(low, b_ref[...])
    part[...] = gram.reshape(part.shape)
    pl.semaphore_wait(barrier, n - 1)

    def scatter(t, _):
        peer = lax.rem(me + t, n)
        pltpu.make_async_remote_copy(
            src_ref=part.at[peer],
            dst_ref=arrived.at[me],
            send_sem=sems.at[0],
            recv_sem=sems.at[1],
            device_id={"space": peer},
            device_id_type=MESH,
        ).start()
        return 0

    lax.fori_loop(1, n, scatter, 0)
    arrived[me] = part[me]
    whole = arrived.at[pl.ds(0, n - 1)]
    pltpu.make_async_copy(whole, whole, sems.at[1]).wait()
    total[...] = jnp.sum(arrived[...], axis=0)

    def gather(t, _):
        peer = lax.rem(me + t, n)
        pltpu.make_async_remote_copy(
            src_ref=total,
            dst_ref=gathered.at[me],
            send_sem=sems.at[2],
            recv_sem=sems.at[3],
            device_id={"space": peer},
            device_id_type=MESH,
        ).start()
        return 0

    lax.fori_loop(1, n, gather, 0)
    gathered[me] = total[...]
    pltpu.make_async_copy(whole, whole, sems.at[0]).wait()
    other = gathered.at[pl.ds(0, n - 1)]
    pltpu.make_async_copy(other, other, sems.at[2]).wait()
    pltpu.make_async_copy(other, other, sems.at[3]).wait()
    out_ref[...] = gathered[...].reshape(out_ref.shape)


def space_gram(a, b, weight):
    n = lax.axis_size("space")
    rank = a.shape[1]
    chunk = (n, rank // n, rank)
    return pl.pallas_call(
        reduce_gram,
        out_shape=jax.ShapeDtypeStruct((rank, rank), F32),
        in_specs=[pl.BlockSpec(memory_space=pltpu.VMEM)] * 3,
        out_specs=pl.BlockSpec(memory_space=pltpu.VMEM),
        scratch_shapes=[
            pltpu.VMEM(chunk, F32),
            pltpu.VMEM(chunk, F32),
            pltpu.VMEM(chunk[1:], F32),
            pltpu.VMEM(chunk, F32),
            pltpu.SemaphoreType.DMA((4,)),
        ],
        compiler_params=pltpu.CompilerParams(
            collective_id=0, has_side_effects=True, vmem_limit_bytes=VMEM_LIMIT
        ),
        name="space_gram",
    )(a, b, weight)


def first_kernel(x_ref, g_ref, out_ref, z, aq):
    chol_inv(g_ref, z, aq)
    high, low = split(z[...])
    out_ref[...] = (mm(x_ref[...], high, NT) + mm(x_ref[...], low, NT)).astype(BF16)


def merge_kernel(lo_ref, hi_ref, b_ref, om_ref, out_ref, m, z, aq):
    rank = b_ref.shape[0]
    oa, ob = om_ref[:rank, :], om_ref[rank:, :]
    bh, bl = split(b_ref[...])
    cross = mm3(jnp.transpose(oa).astype(F32), mm(bh, ob) + mm(bl, ob))
    z[...] = cross
    m[...] = mm(om_ref[...], om_ref[...], TN)
    m[...] = m[...] + z[...] + jnp.transpose(z[...])
    chol_inv(m, z, aq)
    sketch = mm(lo_ref[...], oa) + mm(hi_ref[...], ob)
    out_ref[...] = mm3(sketch, z[...], NT).astype(BF16)


def local_call(body, shape, scratch, name):
    return pl.pallas_call(
        body,
        out_shape=jax.ShapeDtypeStruct(shape, BF16),
        scratch_shapes=scratch,
        compiler_params=pltpu.CompilerParams(vmem_limit_bytes=VMEM_LIMIT),
        name=name,
    )


def shifted(block, axis, distance):
    devices = range(lax.axis_size(axis))
    route = [(i - distance, i) for i in devices if i - distance in devices]
    return lax.ppermute(block, axis, route)


def on_device(snapshots, cell_volume, counts, rim_rows, jac_cols, jacobian, omega):
    rows, rank = snapshots.shape
    blocks = rows // BLOCK
    total = rows * lax.axis_size("space")
    block_index = lax.broadcasted_iota(jnp.int32, (blocks, BLOCK), 0).reshape(rows)
    valid = block_index < counts[0]
    weight = jnp.where(valid, cell_volume / total, 0.0).reshape(1, rows)
    local = jnp.where(valid[:, None], snapshots, 0)
    square = pltpu.VMEM((rank, rank), F32)
    wide = pltpu.VMEM((rank // 2, rank), F32)
    gram = space_gram(local, local, weight)
    current = local_call(first_kernel, (rows, rank), [square, wide], "orthonormal")(local, gram)
    position = lax.axis_index("snap")
    for level in range(LEVELS):
        step = 1 << level
        partner = [(i, i ^ step) for i in range(lax.axis_size("snap"))]
        incoming = lax.ppermute(current, "snap", partner)
        upper = position // step % 2 == 1
        lower_base = jnp.where(upper, incoming, current)
        higher_base = jnp.where(upper, current, incoming)
        cross = space_gram(lower_base, higher_base, weight)
        current = local_call(merge_kernel, (rows, rank), [square, square, wide], "merge")(
            lower_base, higher_base, cross, omega[level]
        )
    blocked = current.reshape(blocks, BLOCK, rank)
    rims = jnp.take(blocked, rim_rows[0], axis=0)
    before = shifted(rims[1], "space", 1)
    after = shifted(rims[0], "space", -1)
    extended = jnp.concatenate([blocked, before[None], after[None]], 0)
    picked = jnp.take(extended, jac_cols, axis=0)
    matrix = jacobian.reshape(blocks, BLOCK, NNZ, BLOCK)
    product = jnp.einsum("bikj,bkjr->bir", matrix, picked, preferred_element_type=F32)
    product = jnp.where(valid[:, None], product.reshape(rows, rank), 0.0)
    return (current, product.astype(BF16))


def solution(mesh):
    in_specs = (
        P("space", "snap"),
        P("space"),
        P("space"),
        P("space", None),
        P("space", None),
        P("space", None),
        P(),
    )
    out_specs = (P("space", "snap"), P("space", "snap"))
    return jax.shard_map(
        on_device, mesh=mesh, in_specs=in_specs, out_specs=out_specs, check_vma=False
    )
```

time: 784 us -> 186 us (0.24)
  the two profiles are of different devices: /device:TPU:98 before, /device:TPU:2 now
where the time goes in v1:
time: 186 us
  Pallas kernels  90.9 us (49%)
  waiting for transfers between devices  56.6 us (30%)
  local copies, waits for them, and re-layouts  14.3 us (8%)
  starting transfers between devices  11.9 us (6%)
  matrix products  5.53 us (3%)
  other arithmetic  4.84 us (3%)
    ppermute x2, waiting for transfers between devices, on_device(): incoming = lax.ppermute(current, 'snap', partner)  54.4 us
    pallas_call x3, Pallas kernels, space_gram(): pl.pallas_call(reduce_gram, out_shape=jax.ShapeDtypeStruct((rank, rank),...  54.4 us
    pallas_call x2, Pallas kernels, on_device(): local_call(merge_kernel, (rows, rank), [square, square, wide], 'merge')  25.7 us
    pallas_call x1, Pallas kernels, on_device(): local_call(first_kernel, (rows, rank), [square, wide], 'orthonormal')  10.8 us
    gather x1, local copies, waits for them, and re-layouts, on_device(): picked = jnp.take(extended, jac_cols, axis=0)  8.06 us
    ppermute x2, starting transfers between devices, shifted(): return lax.ppermute(block, axis, route)  7.33 us
    dot_general x1, matrix products, on_device(): jnp.einsum('bikj,bkjr->bir', matrix, picked, preferred_element_type=F32)  5.53 us
    ppermute x2, starting transfers between devices, on_device(): incoming = lax.ppermute(current, 'snap', partner)  4.57 us
  transfers between devices with their start and end apart: 4, of which 3 were waited for; matrix products, arithmetic and copies ran while one was open for 2% of the time, Pallas kernels for 0%

profile of v1, /device:TPU:2, one launch (start us, length us, event | category | flops | bytes accessed | tf_op | source)
XLA Modules:
  0.0 185.5 jit_solution(8094177588471705724)
XLA Ops:
  1.4 0.7 multiply_select_fusion
  2.1 1.4 broadcast_select_fusion.a_ref.b_ref.x_ref
  3.5 19.8 %space_gram.3.g_ref = f32[256,256]{1,0:T(8,128)S(1)} custom-call(bf16[1536,256]{1,0:T(8,128)(2,1)S(1)} %broadcast_select_fusion.a_ref.b_ref.x_ref, bf16[1536,256]{1,0:T(8,128)(2,1)S(1)} %broadcast_select_fusion.a_ref.b_ref.x_ref, f32[1,1536]{1,0:T(1,128)S(1)} %reshape.63.w_ref), custom_call_target="tpu_custom_call" | custom-call | tf_op jit(solution)/shard_map/space_gram/pallas_call | solution.py:151
  23.3 10.8 %orthonormal.1 = bf16[1536,256]{1,0:T(8,128)(2,1)S(1)} custom-call(bf16[1536,256]{1,0:T(8,128)(2,1)S(1)} %broadcast_select_fusion.a_ref.b_ref.x_ref, f32[256,256]{1,0:T(8,128)S(1)} %space_gram.3.g_ref), custom_call_target="tpu_custom_call" | custom-call | tf_op jit(solution)/shard_map/orthonormal/pallas_call | solution.py:216
  34.1 1.9 %collective-permute-start = (bf16[1536,256]{1,0:T(8,128)(2,1)S(1)}, bf16[1536,256]{1,0:T(8,128)(2,1)S(1)}, u32[]{:S(2)}, u32[]{:S(2)}) collective-permute-start(bf16[1536,256]{1,0:T(8,128)(2,1)S(1)} %orthonormal.1), channel_id=1, source_target_pairs={{0,32},{32,0},{64,96},{96,64},{128,160},{160,128},{192,224},{224,1... | collective-permute-start | bytes 2359304 | tf_op jit(solution)/shard_map/ppermute | solution.py:221
  36.0 1.1 slice_bitcast_fusion
  37.1 18.4 %collective-permute-done = bf16[1536,256]{1,0:T(8,128)(2,1)S(1)} collective-permute-done((bf16[1536,256]{1,0:T(8,128)(2,1)S(1)}, bf16[1536,256]{1,0:T(8,128)(2,1)S(1)}, u32[]{:S(2)}, u32[]{:S(2)}) %collective-permute-start) | collective-permute-done | bytes 786464 | tf_op jit(solution)/shard_map/ppermute | solution.py:221
  55.6 0.1 broadcast_select_fusion.1
  55.7 17.5 %space_gram.4.b_ref = f32[256,256]{1,0:T(8,128)S(1)} custom-call(bf16[1536,256]{1,0:T(8,128)(2,1)S(1)} %get-tuple-element.5.a_ref.lo_ref, bf16[1536,256]{1,0:T(8,128)(2,1)S(1)} %get-tuple-element.4.b_ref.hi_ref, f32[1,1536]{1,0:T(1,128)S(1)} %reshape.63.w_ref), custom_call_target="tpu_custom_call" | custom-call | tf_op jit(solution)/shard_map/space_gram/pallas_call | solution.py:151
  73.2 12.4 %merge.2 = bf16[1536,256]{1,0:T(8,128)(2,1)S(1)} custom-call(bf16[1536,256]{1,0:T(8,128)(2,1)S(1)} %get-tuple-element.5.a_ref.lo_ref, bf16[1536,256]{1,0:T(8,128)(2,1)S(1)} %get-tuple-element.4.b_ref.hi_ref, f32[256,256]{1,0:T(8,128)S(1)} %space_gram.4.b_ref, bf16[512,256]{1,0:T(8,128)(2,1)S(1)} %get-tuple-element.7.om_ref), custom_call_target="tpu_custom_call" | custom-call | tf_op jit(solution)/shard_map/merge/pallas_call | solution.py:226
  85.6 2.7 %collective-permute-start.1 = (bf16[1536,256]{1,0:T(8,128)(2,1)S(1)}, bf16[1536,256]{1,0:T(8,128)(2,1)S(1)}, u32[]{:S(2)}, u32[]{:S(2)}) collective-permute-start(bf16[1536,256]{1,0:T(8,128)(2,1)S(1)} %merge.2), channel_id=1, source_target_pairs={{0,64},{32,96},{64,0},{96,32},{128,192},{160,224},{192,128},{224,1... | collective-permute-start | bytes 2359304 | tf_op jit(solution)/shard_map/ppermute | solution.py:221
  88.5 35.9 %collective-permute-done.1 = bf16[1536,256]{1,0:T(8,128)(2,1)S(1)} collective-permute-done((bf16[1536,256]{1,0:T(8,128)(2,1)S(1)}, bf16[1536,256]{1,0:T(8,128)(2,1)S(1)}, u32[]{:S(2)}, u32[]{:S(2)}) %collective-permute-start.1) | collective-permute-done | bytes 786464 | tf_op jit(solution)/shard_map/ppermute | solution.py:221
  124.5 0.1 broadcast_select_fusion.3
  124.6 17.1 %space_gram.5.b_ref = f32[256,256]{1,0:T(8,128)S(1)} custom-call(bf16[1536,256]{1,0:T(8,128)(2,1)S(1)} %get-tuple-element.3.a_ref.lo_ref, bf16[1536,256]{1,0:T(8,128)(2,1)S(1)} %get-tuple-element.2.b_ref.hi_ref, f32[1,1536]{1,0:T(1,128)S(1)} %reshape.63.w_ref), custom_call_target="tpu_custom_call" | custom-call | tf_op jit(solution)/shard_map/space_gram/pallas_call | solution.py:151
  141.7 13.3 %merge.3 = bf16[1536,256]{1,0:T(8,128)(2,1)} custom-call(bf16[1536,256]{1,0:T(8,128)(2,1)S(1)} %get-tuple-element.3.a_ref.lo_ref, bf16[1536,256]{1,0:T(8,128)(2,1)S(1)} %get-tuple-element.2.b_ref.hi_ref, f32[256,256]{1,0:T(8,128)S(1)} %space_gram.5.b_ref, bf16[512,256]{1,0:T(8,128)(2,1)S(1)} %get-tuple-element.6.om_ref), custom_call_target="tpu_custom_call" | custom-call | tf_op jit(solution)/shard_map/merge/pallas_call | solution.py:226
  155.0 1.7 gather_fusion
  156.8 5.4 %collective-permute-start.3 = (bf16[64,256]{1,0:T(8,128)(2,1)S(1)}, bf16[64,256]{1,0:T(8,128)(2,1)S(1)}, u32[]{:S(2)}, u32[]{:S(2)}) collective-permute-start(bf16[64,256]{1,0:T(8,128)(2,1)S(1)} %get-tuple-element.9), channel_id=1, source_target_pairs={{1,0},{2,1},{3,2},{4,3},{5,4},{6,5},{7,6},{8,7},{9,8},{10,9},{11,1... | collective-permute-start | bytes 98312 | tf_op jit(solution)/shard_map/ppermute | solution.py:202
  162.2 1.9 %collective-permute-start.2 = (bf16[64,256]{1,0:T(8,128)(2,1)S(1)}, bf16[64,256]{1,0:T(8,128)(2,1)S(1)}, u32[]{:S(2)}, u32[]{:S(2)}) collective-permute-start(bf16[64,256]{1,0:T(8,128)(2,1)S(1)} %get-tuple-element.8), channel_id=1, source_target_pairs={{0,1},{1,2},{2,3},{3,4},{4,5},{5,6},{6,7},{7,8},{8,9},{9,10},{10,1... | collective-permute-start | bytes 98312 | tf_op jit(solution)/shard_map/ppermute | solution.py:202
  164.1 3.1 %reshape.65 = bf16[24,64,8,64]{3,2,1,0:T(8,128)(2,1)} reshape(bf16[1536,512]{1,0:T(8,128)(2,1)S(1)} %copy-done) | data formatting | bytes 3145728 | tf_op jit(solution)/shard_map/reshape | solution.py:235
  167.3 2.2 %collective-permute-done.2 = bf16[64,256]{1,0:T(8,128)(2,1)S(1)} collective-permute-done((bf16[64,256]{1,0:T(8,128)(2,1)S(1)}, bf16[64,256]{1,0:T(8,128)(2,1)S(1)}, u32[]{:S(2)}, u32[]{:S(2)}) %collective-permute-start.2) | collective-permute-done | bytes 32800 | tf_op jit(solution)/shard_map/ppermute | solution.py:202
  169.5 1.2 pad_maximum_fusion
  170.8 8.1 %gather_fusion.1 = bf16[192,64,256]{2,1,0:T(8,128)(2,1)} fusion(bf16[26,64,256]{2,1,0:T(8,128)(2,1)S(1)} %pad_maximum_fusion, s32[1024]{0:T(1024)S(1)} %pad_clamp_fusion), kind=kCustom, calls=%fused_computation.1 | custom fusion | bytes 12583680 | tf_op jit(solution)/shard_map/jit(_take)/gather | solution.py:234
  178.8 5.5 %fusion = bf16[24,256,64,1]{1,2,3,0:T(8,128)(2,1)S(1)} fusion(bf16[24,8,64,256]{3,2,1,0:T(8,128)(2,1)} %bitcast.29, pred[24,8]{1,0:T(8,128)(4,1)S(1)} %copy.11, bf16[24,64,8,64]{3,2,1,0:T(8,128)(2,1)} %reshape.65), kind=kOutput, calls=%fused_computation.2 | convolution fusion | flops 405798912 | bytes 8650944 | tf_op jit(solution)/shard_map/bikj,bkjr->bir/dot_general | solution.py:236
  184.4 1.2 fusion.5
  (21 shorter events, 0.5 us)
Async XLA Ops:
  3.5 84.8 %copy-start.1 = (s32[24,8]{0,1:T(8,128)S(1)}, s32[24,8]{0,1:T(8,128)}, u32[]{:S(2)}) copy-start(s32[24,8]{0,1:T(8,128)} %param.11) | copy-start | bytes 2308
  3.5 85.0 %copy-start.2 = (s32[1,2]{1,0:T(1,128)S(1)}, s32[1,2]{1,0:T(1,128)}, u32[]{:S(2)}) copy-start(s32[1,2]{1,0:T(1,128)} %param.10) | copy-start | bytes 28
  34.1 21.5 %collective-permute-start = (bf16[1536,256]{1,0:T(8,128)(2,1)S(1)}, bf16[1536,256]{1,0:T(8,128)(2,1)S(1)}, u32[]{:S(2)}, u32[]{:S(2)}) collective-permute-start(bf16[1536,256]{1,0:T(8,128)(2,1)S(1)} %orthonormal.1), channel_id=1, source_target_pairs={{0,32},{32,0},{64,96},{96,64},{128,160},{160,128},{192,224},{224,1... | collective-permute-start | bytes 2359304 | tf_op jit(solution)/shard_map/ppermute | solution.py:221
  55.7 108.5 %copy-start = (bf16[1536,512]{1,0:T(8,128)(2,1)S(1)}, bf16[1536,512]{1,0:T(8,128)(2,1)}, u32[]{:S(2)}) copy-start(bf16[1536,512]{1,0:T(8,128)(2,1)} %param.12) | copy-start | bytes 4718596
  85.6 38.9 %collective-permute-start.1 = (bf16[1536,256]{1,0:T(8,128)(2,1)S(1)}, bf16[1536,256]{1,0:T(8,128)(2,1)S(1)}, u32[]{:S(2)}, u32[]{:S(2)}) collective-permute-start(bf16[1536,256]{1,0:T(8,128)(2,1)S(1)} %merge.2), channel_id=1, source_target_pairs={{0,64},{32,96},{64,0},{96,32},{128,192},{160,224},{192,128},{224,1... | collective-permute-start | bytes 2359304 | tf_op jit(solution)/shard_map/ppermute | solution.py:221
  156.8 10.6 %collective-permute-start.3 = (bf16[64,256]{1,0:T(8,128)(2,1)S(1)}, bf16[64,256]{1,0:T(8,128)(2,1)S(1)}, u32[]{:S(2)}, u32[]{:S(2)}) collective-permute-start(bf16[64,256]{1,0:T(8,128)(2,1)S(1)} %get-tuple-element.9), channel_id=1, source_target_pairs={{1,0},{2,1},{3,2},{4,3},{5,4},{6,5},{7,6},{8,7},{9,8},{10,9},{11,1... | collective-permute-start | bytes 98312 | tf_op jit(solution)/shard_map/ppermute | solution.py:202
  162.2 7.3 %collective-permute-start.2 = (bf16[64,256]{1,0:T(8,128)(2,1)S(1)}, bf16[64,256]{1,0:T(8,128)(2,1)S(1)}, u32[]{:S(2)}, u32[]{:S(2)}) collective-permute-start(bf16[64,256]{1,0:T(8,128)(2,1)S(1)} %get-tuple-element.8), channel_id=1, source_target_pairs={{0,1},{1,2},{2,3},{3,4},{4,5},{5,6},{6,7},{7,8},{8,9},{9,10},{10,1... | collective-permute-start | bytes 98312 | tf_op jit(solution)/shard_map/ppermute | solution.py:202

commit v2 on v1

v2 whole, which is shorter than its diff:
```python
import functools

import jax
import jax.numpy as jnp
from jax import lax
from jax.experimental import pallas as pl
from jax.experimental.pallas import tpu as pltpu
from jax.sharding import PartitionSpec as P

BLOCK = 64
NNZ = 8
LEVELS = 2
F32, BF16 = jnp.float32, jnp.bfloat16
NN = ((1,), (0,))
NT = ((1,), (1,))
TN = ((0,), (0,))
MESH = pl.DeviceIdType.MESH
VMEM_LIMIT = 48 * 1024 * 1024


def split(a):
    hi = a.astype(BF16)
    return hi, (a - hi.astype(F32)).astype(BF16)

def mm(a, b, dims=((1,), (0,))):
    return lax.dot_general(a, b, (dims, ((), ())), preferred_element_type=F32)


def mm3(a, b, dims=NN):
    ah, al = split(a)
    bh, bl = split(b)
    return mm(ah, bh, dims) + (mm(ah, bl, dims) + mm(al, bh, dims))

def leaf(aq, W=32):
    T = W // 8
    def panel(k, _):
        r0 = pl.multiple_of(k * W, W)
        rows = aq[pl.ds(r0, W), :]
        diag = pltpu.roll(rows[:, :128], lax.rem(128 - r0, 128), axis=1)
        C = [[jnp.broadcast_to(diag[8*t:8*t+8, m:m+1], (8, 128)) for t in range(T)] for m in range(W)]
        lane = lax.broadcasted_iota(jnp.int32, (8, 128), 1)
        sub = lax.broadcasted_iota(jnp.int32, (8, 128), 0)
        E = [(lane == sub + 8*t).astype(F32) for t in range(T)]
        scale = [jnp.zeros((8, 128), F32) for t in range(T)]
        for j in range(W):
            tj, sj = divmod(j, 8)
            piv = jnp.broadcast_to(C[j][tj][sj:sj+1, :], (8, 128))
            r = pl.reciprocal(piv, approx=True)
            f = [None]*T
            for t in range(tj, T):
                f[t] = C[j][t] * r
            f[tj] = jnp.where(sub > sj, f[tj], 0.0)
            for m in range(j + 1, W):
                tm, sm = divmod(m, 8)
                c = jnp.broadcast_to(C[j][tm][sm:sm+1, :], (8, 128))
                for t in range(tm, T):
                    C[m][t] = C[m][t] - f[t] * c
            e = jnp.broadcast_to(E[tj][sj:sj+1, :], (8, 128))
            for t in range(tj, T):
                E[t] = E[t] - f[t] * e
            scale[tj] = jnp.where(sub == sj, piv, scale[tj])
        E = [E[t] * lax.rsqrt(scale[t]) for t in range(T)]
        inv = jnp.concatenate(E, 0)[:, :W]
        R = mm3(inv, rows)
        low = jnp.transpose(R[:, :128])
        low = jnp.where(lax.broadcasted_iota(jnp.int32, low.shape, 0) >= r0 + W, low, 0.0)
        aq[...] = aq[...] - mm3(low, R)
        aq[pl.ds(r0, W), :] = R
        return 0
    lax.fori_loop(0, 128 // W, panel, 0)

def chol_upper(a, z, aq):
    ident = eye(128)
    aq[:, 128:] = ident
    aq[:, :128] = a[:128, :128]
    leaf(aq)
    z11 = aq[:, 128:]
    z[:128, :128] = z11
    l21 = mm3(a[128:, :128], z11, NT)
    aq[:, :128] = a[128:, 128:] - mm3(l21, l21, NT)
    aq[:, 128:] = ident
    z[128:, :128] = mm3(l21, z11)


def chol_lower(z, aq):
    leaf(aq)
    z22 = aq[:, 128:]
    z[128:, 128:] = z22
    z[128:, :128] = -mm3(z22, z[128:, :128])
    z[:128, 128:] = jnp.zeros((128, 128), F32)


def chol_inv(a, z, aq):
    chol_upper(a, z, aq)
    chol_lower(z, aq)


def iota(shape, dim):
    return lax.broadcasted_iota(jnp.int32, shape, dim)


def eye(n):
    return (iota((n, n), 0) == iota((n, n), 1)).astype(F32)


def mm3s(a, b, dims=NN):
    return mm(a[0], b[0], dims) + (mm(a[0], b[1], dims) + mm(a[1], b[0], dims))


def mm2(a, b, dims=NN):
    high, low = split(a)
    return mm(high, b, dims) + mm(low, b, dims)


def mm2r(a, b, dims=NN):
    high, low = split(b)
    return mm(a, high, dims) + mm(a, low, dims)


def newton_step(a_ref, z_ref):
    a = a_ref[...]
    row, col = iota(a.shape, 0), iota(a.shape, 1)
    h = split(jnp.where(row > col, -a, jnp.where(row == col, 1.5 - 0.5 * a, 0.0)))
    t = mm3s(h, split(a))
    z = mm3s(h, split(z_ref[...]))
    a_ref[...] = mm3s(split(t), h, NT)
    z_ref[...] = z


def residual(a, count):
    worst = jnp.float32(0.0)
    for i in range(count):
        off = a[i] - eye(a.shape[1])
        total = jnp.sum(off * off)
        worst = jnp.maximum(worst, jnp.where(total < 1e30, total, 1e30))
    return worst


def factor(a, z, first, start, wide, count, fixed, most):
    for i in range(count):
        first[i] = a[i]
        start[i] = z[i]
    for _ in range(fixed):
        for i in range(count):
            newton_step(a.at[i], z.at[i])

    def unsettled(state):
        return jnp.logical_and(state[0] < most, state[1] > 1e-7)

    def again(state):
        for i in range(count):
            newton_step(a.at[i], z.at[i])
        return state[0] + 1, residual(a, count)

    left = lax.while_loop(unsettled, again, (jnp.int32(fixed), residual(a, count)))[1]

    @pl.when(left > 1e-7)
    def _():
        def direct(i, _):
            chol_inv(first.at[i], z.at[i], wide)
            z[i] = mm3(z[i], start[i])
            return 0

        lax.fori_loop(0, count, direct, 0)


class Phases:
    def __init__(self, sends, arrivals):
        self.sends, self.arrivals = sends, arrivals
        self.flying = []
        me = lax.axis_index("space")
        self.core = lax.rem(me, 2)
        self.y = lax.rem(me // 2, 4)
        self.x = me // 8
        self.snap = lax.axis_index("snap")
        self.place = lax.rem(self.snap, 4)
        self.used = 0

    def space(self, x, y, core):
        return (x * 4 + y) * 2 + core

    def peers(self):
        found = [{"space": self.space(self.x, self.y, 1 - self.core)}]
        for d in (1, 2, 3):
            found.append({"space": self.space(lax.rem(self.x + d, 4), self.y, self.core)})
            found.append({"space": self.space(self.x, lax.rem(self.y + d, 4), self.core)})
            found.append({"snap": self.other(d)})
        return found

    def other(self, d):
        place = self.place
        if d & 1:
            place = place + 1 - 2 * lax.rem(place, 2)
        if d & 2:
            place = place + 2 - 4 * (place // 2)
        return self.snap - self.place + place

    def send(self, src, dst, device):
        slot = self.used
        self.used += 1
        copy = pltpu.make_async_remote_copy(
            src_ref=src,
            dst_ref=dst,
            send_sem=self.sends.at[slot],
            recv_sem=self.arrivals.at[slot],
            device_id=device,
            device_id_type=MESH,
        )
        copy.start()
        self.flying.append(copy)
        return copy

    def finish(self):
        for copy in self.flying:
            copy.wait_send()

    def greet(self, devices):
        barrier = pltpu.get_barrier_semaphore()
        for device in devices:
            pl.semaphore_signal(barrier, inc=1, device_id=device, device_id_type=MESH)

    def met(self, count):
        pl.semaphore_wait(pltpu.get_barrier_semaphore(), count)

    def along(self, half, major, d):
        if (half == 0) == major:
            place = lax.rem(self.x + d, 4)
            return place, {"space": self.space(place, self.y, self.core)}
        place = lax.rem(self.y + d, 4)
        return place, {"space": self.space(self.x, place, self.core)}

    def own(self, half, major):
        return self.x if (half == 0) == major else self.y


def rows_of(place, size):
    return pl.ds(pl.multiple_of(place * size, size), size)


def sum_over_space(ph, part, bc, bx, by, s1, s2, s3, spread, beside=None):
    copy = ph.send(
        part.at[:, :, rows_of(1 - ph.core, 128), :],
        bc,
        {"space": ph.space(ph.x, ph.y, 1 - ph.core)},
    )
    copy.wait_recv()
    s1[...] = part[:, :, rows_of(ph.core, 128), :] + bc[...]
    copies = []
    for d in (1, 2, 3):
        for half in (0, 1):
            place, device = ph.along(half, True, d)
            copies.append(ph.send(s1.at[half, :, rows_of(place, 32), :], bx.at[half, d - 1], device))
    if beside is not None:
        beside()
    for copy in copies:
        copy.wait_recv()
    for half in (0, 1):
        mine = s1[half, :, rows_of(ph.own(half, True), 32), :]
        s2[half] = mine + (bx[half, 0] + bx[half, 1] + bx[half, 2])
    copies = []
    for d in (1, 2, 3):
        for half in (0, 1):
            place, device = ph.along(half, False, d)
            copies.append(ph.send(s2.at[half, :, rows_of(place, 8), :], by.at[half, d - 1], device))
    for copy in copies:
        copy.wait_recv()
    for half in (0, 1):
        mine = s2[half, :, rows_of(ph.own(half, False), 8), :]
        s3[half] = mine + (by[half, 0] + by[half, 1] + by[half, 2])
    copies = []
    for d in (1, 2, 3):
        copies.append(ph.send(s3, spread.at[d], {"snap": ph.other(d)}))
    spread[0] = s3[...]
    for copy in copies:
        copy.wait_recv()


def give_over_space(ph, chunk, g1, g2, out):
    copies = []
    for half in (0, 1):
        mine = rows_of(ph.own(half, False), 8)
        for d in (1, 2, 3):
            _, device = ph.along(half, False, d)
            copies.append(ph.send(chunk.at[half], g1.at[half, :, mine, :], device))
        g1[half, :, mine, :] = chunk[half]
    for copy in copies:
        copy.wait_recv()
    copies = []
    for half in (0, 1):
        mine = rows_of(ph.own(half, True), 32)
        for d in (1, 2, 3):
            _, device = ph.along(half, True, d)
            copies.append(ph.send(g1.at[half], g2.at[half, :, mine, :], device))
        g2[half, :, mine, :] = g1[half]
    for copy in copies:
        copy.wait_recv()
    mine = rows_of(ph.core, 128)
    copy = ph.send(
        g2, out.at[:, :, mine, :], {"space": ph.space(ph.x, ph.y, 1 - ph.core)}
    )
    out[:, :, mine, :] = g2[...]
    copy.wait_recv()


def put_halves(ref, index, square):
    ref[0, index] = square[:, :128]
    ref[1, index] = square[:, 128:]


def whole(ref, index):
    return jnp.concatenate([ref[0, index], ref[1, index]], axis=1)


def quarter_rows(place, size):
    return rows_of(2 * lax.rem(place, 2) + place // 2, size)


def first_sum(
    x_ref, w_ref, om_ref, out_ref, parts_ref, zo_ref,
    part, bc, bx, by, s1, s2, s3, spread, chunk, g1, g2, got, sends, arrivals, parts, m, zo, wide
):
    ph = Phases(sends, arrivals)
    ph.greet(ph.peers())
    weighted = jnp.transpose(x_ref[...]).astype(F32) * w_ref[...]
    put_halves(part, 0, mm2(weighted, x_ref[...]))
    ph.met(10)
    quarter = parts.shape[1]

    def give_rows(d):
        there = ph.other(d)
        rows = quarter_rows(lax.rem(there, 4), quarter)
        return ph.send(x_ref.at[rows, :], parts.at[d - 1], {"snap": there})

    bulk = [give_rows(2), give_rows(1)]
    om = om_ref[ph.core]
    m[...] = mm(om, om, TN)
    mine = zo.at[ph.core]
    sum_over_space(
        ph, part, bc, bx, by, s1, s2, s3, spread, lambda: chol_upper(m, mine, wide)
    )
    bulk.append(give_rows(3))
    for d in range(4):
        chunk[:, d] = spread[d, :, 0]
    give_over_space(ph, chunk, g1, g2, got)
    chol_lower(mine, wide)
    factor_copy = ph.send(mine, mine, {"space": ph.space(ph.x, ph.y, 1 - ph.core)})
    for d in range(4):
        out_ref[d] = whole(got, d)
    for copy in bulk:
        copy.wait_recv()
    parts_ref[...] = parts[...]
    factor_copy.wait_recv()
    zo_ref[...] = zo[...]
    ph.finish()


def second_sum(part, out_ref, bc, bx, by, s1, s2, s3, spread, chunk, g1, g2, got, sends, arrivals):
    ph = Phases(sends, arrivals)
    ph.greet(ph.peers())
    ph.met(10)
    sum_over_space(ph, part, bc, bx, by, s1, s2, s3, spread)
    chunk[...] = (spread[0] + spread[1]) + (spread[2] + spread[3])
    give_over_space(ph, chunk, g1, g2, got)
    for d in range(3):
        out_ref[d] = whole(got, d)
    ph.finish()


def sum_scratch(before, after, copies=29):
    return [
        pltpu.VMEM((2, before, 128, 128), F32),
        pltpu.VMEM((2, 3, before, 32, 128), F32),
        pltpu.VMEM((2, 3, before, 8, 128), F32),
        pltpu.VMEM((2, before, 128, 128), F32),
        pltpu.VMEM((2, before, 32, 128), F32),
        pltpu.VMEM((2, before, 8, 128), F32),
        pltpu.VMEM((4, 2, before, 8, 128), F32),
        pltpu.VMEM((2, after, 8, 128), F32),
        pltpu.VMEM((2, after, 32, 128), F32),
        pltpu.VMEM((2, after, 128, 128), F32),
        pltpu.VMEM((2, after, 256, 128), F32),
        pltpu.SemaphoreType.DMA((copies,)),
        pltpu.SemaphoreType.DMA((copies,)),
    ]


def basis_kernel(place_ref, g_ref, x0, xs, w_ref, om_ref, sk_ref, part_ref, a, z, first, start, wide, base):
    place = place_ref[0]
    rank = om_ref.shape[2]
    diagonal = iota((rank, rank), 0) == iota((rank, rank), 1)
    for d in range(4):
        g = g_ref[d]
        pivots = jnp.where(diagonal, g, 0.0)
        down = lax.rsqrt(jnp.sum(pivots, axis=1, keepdims=True))
        across = lax.rsqrt(jnp.sum(pivots, axis=0, keepdims=True))
        a[d] = g * down * across
        z[d] = jnp.where(diagonal, down, 0.0)
    factor(a, z, first, start, wide, 4, 3, 8)
    for d in range(4):
        x = x0[...] if d == 0 else xs[d - 1]
        base[place ^ d] = mm2r(x, z[d], NT).astype(BF16)
    weight = w_ref[...]
    for pair in (0, 1):
        low, high = base[2 * pair], base[2 * pair + 1]
        sketch = mm(low, om_ref[0, :rank, :]) + mm(high, om_ref[0, rank:, :])
        sk_ref[:, pair * rank : (pair + 1) * rank] = sketch.astype(BF16)
        put_halves(part_ref, pair, mm2(jnp.transpose(low).astype(F32) * weight, high))
    low, high = sk_ref[:, :rank], sk_ref[:, rank:]
    put_halves(part_ref, 2, mm2(jnp.transpose(low).astype(F32) * weight, high))


def near_identity(z, om, cross, a, t):
    rank = cross.shape[0]
    qa = mm2(z, om[:rank], NT)
    qb = mm2r(om[rank:], z, NT)
    t[...] = mm3(qa, mm3(cross, qb))
    a[...] = eye(rank) + t[...] + jnp.transpose(t[...])


def final_kernel(c_ref, om_ref, zo_ref, sk_ref, out_ref, a, z, first, start, t, wide):
    rank = om_ref.shape[2]
    for pair in (0, 1):
        near_identity(zo_ref[0], om_ref[0], c_ref[pair], a.at[pair], t.at[pair])
        z[pair] = zo_ref[0]
    factor(a, z, first, start, wide, 2, 3, 8)
    cross = mm3(mm3(z[0], c_ref[2]), z[1], NT)
    near_identity(zo_ref[1], om_ref[1], cross, a.at[2], t.at[0])
    z[2] = zo_ref[1]
    factor(
        a.at[pl.ds(2, 1)], z.at[pl.ds(2, 1)], first, start, wide, 1, 3, 8
    )
    last = z[2]
    for pair in (0, 1):
        u = mm2r(om_ref[1, pair * rank : (pair + 1) * rank, :], last, NT)
        t[pair] = mm3(jnp.transpose(z[pair]), u)
    left, right = split(t[0]), split(t[1])
    low, high = sk_ref[:, :rank], sk_ref[:, rank:]
    final = (mm(low, left[0]) + mm(high, right[0])) + (mm(low, left[1]) + mm(high, right[1]))
    out_ref[...] = final.astype(BF16)


def spread_kernel(rim_ref, own_ref, base_ref, rims_ref, base, rim_out, rim_in, sends, arrivals):
    ph = Phases(sends, arrivals)
    near, far = ph.other(1), ph.other(2)
    me, n = lax.axis_index("space"), lax.axis_size("space")
    before, after = {"space": lax.rem(me + n - 1, n)}, {"space": lax.rem(me + 1, n)}
    ph.greet([{"snap": near}, {"snap": far}, before, after])
    quarter = own_ref.shape[0] // BLOCK
    pieces = 3
    size = quarter // pieces

    def rows(place, piece):
        return pl.ds((2 * lax.rem(place, 2) + place // 2) * quarter + piece * size, size)

    own = own_ref[...].reshape(quarter, BLOCK, own_ref.shape[1])
    for piece in range(pieces):
        base[rows(ph.place, piece)] = own[piece * size : (piece + 1) * size]
    ph.met(4)
    across, relayed = [], []
    for piece in range(pieces):
        mine = base.at[rows(ph.place, piece)]
        across.append(ph.send(mine, mine, {"snap": far}))
    for piece in range(pieces):
        mine = base.at[rows(ph.place, piece)]
        relayed.append(ph.send(mine, mine, {"snap": near}))
    for piece in range(pieces):
        across[piece].wait_recv()
        theirs = base.at[rows(lax.rem(far, 4), piece)]
        relayed.append(ph.send(theirs, theirs, {"snap": near}))
    for copy in relayed:
        copy.wait_recv()
    for side in (0, 1):
        rim_out[side] = base[rim_ref[0, side]]

    swaps = [
        ph.send(rim_out.at[0], rim_in.at[1], before),
        ph.send(rim_out.at[1], rim_in.at[0], after),
    ]
    base_ref[...] = base[...].reshape(base_ref.shape)
    for copy in swaps:
        copy.wait_recv()
    rims_ref[:BLOCK, :] = jnp.where(me > 0, rim_in[0], 0)
    rims_ref[BLOCK:, :] = jnp.where(me < n - 1, rim_in[1], 0)
    ph.finish()


def product_kernel(cols_ref, count_ref, full_ref, rims_ref, jac_ref, base_ref, out_ref, held):
    rows, rank = full_ref.shape
    blocks = rows // BLOCK
    base_ref[...] = full_ref[...]
    held[:rows, :] = full_ref[...]
    held[rows:, :] = rims_ref[...]
    count = count_ref[0]

    def block(b, _):
        here = pl.ds(pl.multiple_of(b * BLOCK, BLOCK), BLOCK)
        picked = [
            held[pl.ds(pl.multiple_of(cols_ref[b, k] * BLOCK, BLOCK), BLOCK), :] for k in range(NNZ)
        ]
        product = mm(jac_ref[here, :], jnp.concatenate(picked, axis=0))
        out_ref[here, :] = jnp.where(b < count, product, 0.0).astype(BF16)
        return 0

    lax.fori_loop(0, blocks, block, 0, unroll=2)


VM = pl.BlockSpec(memory_space=pltpu.VMEM)
SM = pl.BlockSpec(memory_space=pltpu.SMEM)


def call(body, outs, ins, scratch, name, **params):
    return pl.pallas_call(
        body,
        out_shape=outs,
        in_specs=ins,
        out_specs=jax.tree.map(lambda _: VM, outs),
        scratch_shapes=scratch,
        compiler_params=pltpu.CompilerParams(vmem_limit_bytes=VMEM_LIMIT, **params),
        name=name,
    )


def on_device(snapshots, cell_volume, counts, rim_rows, jac_cols, jacobian, omega):
    rows, rank = snapshots.shape
    blocks, quarter = rows // BLOCK, rows // 4
    total = rows * lax.axis_size("space")
    valid = lax.broadcasted_iota(jnp.int32, (blocks, BLOCK), 0).reshape(rows) < counts[0]
    weight = jnp.where(valid, cell_volume / total, 0.0).reshape(1, rows)
    local = jnp.where(valid[:, None], snapshots, 0)
    place = lax.axis_index("snap") % 4
    start = (2 * (place % 2) + place // 2) * quarter
    square = (rank, rank)
    wide = pltpu.VMEM((rank // 2, rank), F32)

    def squares(n):
        return pltpu.VMEM((n, rank, rank), F32)

    grams, others, starts = call(
        first_sum,
        [
            jax.ShapeDtypeStruct((4, rank, rank), F32),
            jax.ShapeDtypeStruct((3, quarter, rank), BF16),
            jax.ShapeDtypeStruct((2, rank, rank), F32),
        ],
        [VM] * 3,
        [pltpu.VMEM((2, 1, rank, rank // 2), F32)]
        + sum_scratch(1, 4, 33)
        + [pltpu.VMEM((3, quarter, rank), BF16), pltpu.VMEM(square, F32), squares(2), wide],
        "first_sum",
        collective_id=0,
        has_side_effects=True,
    )(local, weight, omega)
    sketch, cross = call(
        basis_kernel,
        [
            jax.ShapeDtypeStruct((quarter, 2 * rank), BF16),
            jax.ShapeDtypeStruct((2, 3, rank, rank // 2), F32),
        ],
        [SM] + [VM] * 5,
        [squares(4)] * 4 + [wide, pltpu.VMEM((4, quarter, rank), BF16)],
        "bases",
    )(
        place.reshape(1),
        grams,
        lax.dynamic_slice_in_dim(local, start, quarter, 0),
        others,
        lax.dynamic_slice_in_dim(weight, start, quarter, 1),
        omega,
    )
    cross = call(
        second_sum,
        jax.ShapeDtypeStruct((3, rank, rank), F32),
        [VM],
        sum_scratch(3, 3),
        "second_sum",
        collective_id=1,
        has_side_effects=True,
    )(cross)
    final = call(
        final_kernel,
        jax.ShapeDtypeStruct((quarter, rank), BF16),
        [VM] * 4,
        [squares(3), squares(3), squares(2), squares(2), squares(2), wide],
        "final_rows",
    )(cross, omega, starts, sketch)
    full, rims = call(
        spread_kernel,
        [
            jax.ShapeDtypeStruct((rows, rank), BF16),
            jax.ShapeDtypeStruct((2 * BLOCK, rank), BF16),
        ],
        [SM, VM],
        [
            pltpu.VMEM((blocks, BLOCK, rank), BF16),
            pltpu.VMEM((2, BLOCK, rank), BF16),
            pltpu.VMEM((2, BLOCK, rank), BF16),
            pltpu.SemaphoreType.DMA((11,)),
            pltpu.SemaphoreType.DMA((11,)),
        ],
        "spread_rows",
        collective_id=2,
        has_side_effects=True,
    )(rim_rows, final)
    basis, product = call(
        product_kernel,
        [jax.ShapeDtypeStruct((rows, rank), BF16)] * 2,
        [SM, SM, VM, VM, VM],
        [pltpu.VMEM((rows + 2 * BLOCK, rank), BF16)],
        "jac_product",
    )(jac_cols, counts, full, rims, jacobian)
    return (basis, product)


def solution(mesh):
    in_specs = (
        P("space", "snap"),
        P("space"),
        P("space"),
        P("space", None),
        P("space", None),
        P("space", None),
        P(),
    )
    out_specs = (P("space", "snap"), P("space", "snap"))
    return jax.shard_map(
        on_device, mesh=mesh, in_specs=in_specs, out_specs=out_specs, check_vma=False
    )
```

time: 186 us -> 158 us (0.85)
  the two profiles are of different devices: /device:TPU:2 before, /device:TPU:128 now
where the time goes in v2:
time: 158 us
  Pallas kernels  155 us (98%)
    pallas_call x1, Pallas kernels, on_device(): call(basis_kernel, [jax.ShapeDtypeStruct((quarter, 2 * rank), BF16), jax....  54.5 us
    pallas_call x1, Pallas kernels, on_device(): call(first_sum, [jax.ShapeDtypeStruct((4, rank, rank), F32), jax.ShapeDty...  37.5 us
    pallas_call x1, Pallas kernels, on_device(): call(second_sum, jax.ShapeDtypeStruct((3, rank, rank), F32), [VM], sum_sc...  27 us
    pallas_call x1, Pallas kernels, on_device(): call(spread_kernel, [jax.ShapeDtypeStruct((rows, rank), BF16), jax.ShapeD...  21.2 us
    pallas_call x1, Pallas kernels, on_device(): call(final_kernel, jax.ShapeDtypeStruct((quarter, rank), BF16), [VM] * 4,...  10.2 us
    pallas_call x1, Pallas kernels, on_device(): call(product_kernel, [jax.ShapeDtypeStruct((rows, rank), BF16)] * 2, [SM,...  4.37 us

profile of v2, /device:TPU:128, one launch (start us, length us, event | category | flops | bytes accessed | tf_op | source)
XLA Modules:
  0.0 157.9 jit_solution(7032906155125495171)
XLA Ops:
  0.6 0.0 copy-start.3
  0.6 0.0 copy-start
  1.4 0.1 lt.30
  1.5 1.4 broadcast_select_fusion.x_ref
  2.9 0.0 copy-done.3
  3.0 0.1 dynamic-slice.3
  3.1 0.0 copy-done
  3.1 37.5 %first_sum.1 = (f32[4,256,256]{2,1,0:T(8,128)S(1)}, bf16[3,384,256]{2,1,0:T(8,128)(2,1)S(1)}, f32[2,256,256]{2,1,0:T(8,128)S(1)}) custom-call(bf16[1536,256]{1,0:T(8,128)(2,1)S(1)} %broadcast_select_fusion.x_ref, f32[1,1536]{1,0:T(1,128)S(1)} %reshape.20.w_ref, bf16[2,512,256]{2,1,0:T(8,128)(2,1)S(1)} %copy-done), custom_call_target="tpu_custom_call" | custom-call | tf_op jit(solution)/shard_map/first_sum/pallas_call | solution.py:538
  40.6 54.5 %bases.1 = (bf16[384,512]{1,0:T(8,128)(2,1)S(1)}, f32[2,3,256,128]{3,2,1,0:T(8,128)S(1)}) custom-call(s32[1]{0:T(128)} %bitcast.place_ref, f32[4,256,256]{2,1,0:T(8,128)S(1)} %get-tuple-element.9.g_ref, bf16[384,256]{1,0:T(8,128)(2,1)S(1)} %constant_dynamic-slice_fusion.x0, bf16[3,384,256]{2,1,0:T(8,128)(2,1)S(1)} %get-tuple-element.10.xs, ...), custom_call_target="tpu_custom_call" | custom-call | tf_op jit(solution)/shard_map/bases/pallas_call | solution.py:553
  95.0 27.0 %second_sum.1.c_ref = f32[3,256,256]{2,1,0:T(8,128)S(1)} custom-call(f32[2,3,256,128]{3,2,1,0:T(8,128)S(1)} %get-tuple-element.11.part), custom_call_target="tpu_custom_call" | custom-call | tf_op jit(solution)/shard_map/second_sum/pallas_call | solution.py:570
  122.0 0.0 copy-start.2
  122.0 0.0 copy-start.4
  122.0 0.0 copy-start.1
  122.1 10.2 %final_rows.1.own_ref = bf16[384,256]{1,0:T(8,128)(2,1)S(1)} custom-call(f32[3,256,256]{2,1,0:T(8,128)S(1)} %second_sum.1.c_ref, bf16[2,512,256]{2,1,0:T(8,128)(2,1)S(1)} %copy-done, f32[2,256,256]{2,1,0:T(8,128)S(1)} %get-tuple-element.12.zo_ref, bf16[384,512]{1,0:T(8,128)(2,1)S(1)} %get-tuple-element.13.sk_ref), custom_call_target="tpu_custom_call" | custom-call | tf_op jit(solution)/shard_map/final_rows/pallas_call | solution.py:579
  132.2 0.0 copy-done.2
  132.3 21.2 %spread_rows.1 = (bf16[1536,256]{1,0:T(8,128)(2,1)S(1)}, bf16[128,256]{1,0:T(8,128)(2,1)S(1)}) custom-call(s32[1,2]{1,0:T(1,128)S(1)} %copy-done.2, bf16[384,256]{1,0:T(8,128)(2,1)S(1)} %final_rows.1.own_ref), custom_call_target="tpu_custom_call" | custom-call | tf_op jit(solution)/shard_map/spread_rows/pallas_call | solution.py:586
  153.5 0.0 copy-done.4
  153.5 0.1 copy.9.cols_ref
  153.6 0.0 copy-done.1
  153.6 4.4 %jac_product.1 = (bf16[1536,256]{1,0:T(8,128)(2,1)}, bf16[1536,256]{1,0:T(8,128)(2,1)}) custom-call(s32[24,8]{1,0:T(8,128)S(1)} %copy.9.cols_ref, s32[1]{0:T(128)} %copy.10.count_ref, bf16[1536,256]{1,0:T(8,128)(2,1)S(1)} %get-tuple-element.14.full_ref, bf16[128,256]{1,0:T(8,128)(2,1)S(1)} %get-tuple-element.15.rims_ref, bf16[1536,512]{1,0:T(8,128)(2,1)S(1)} %copy-done.1), custom_call_target="tpu_custom_call" | custom-call | tf_op jit(solution)/shard_map/jac_product/pallas_call | solution.py:604
  (5 shorter events, 0.0 us)
Async XLA Ops:
  0.6 2.3 %copy-start.3 = (f32[1536]{0:T(1024)S(1)}, f32[1536]{0:T(1024)}, u32[]{:S(2)}) copy-start(f32[1536]{0:T(1024)} %param.8) | copy-start | bytes 18436
  0.6 2.4 %copy-start = (bf16[2,512,256]{2,1,0:T(8,128)(2,1)S(1)}, bf16[2,512,256]{2,1,0:T(8,128)(2,1)}, u32[]{:S(2)}) copy-start(bf16[2,512,256]{2,1,0:T(8,128)(2,1)} %om_ref.5) | copy-start | bytes 1572868
  122.0 10.2 %copy-start.2 = (s32[1,2]{1,0:T(1,128)S(1)}, s32[1,2]{1,0:T(1,128)}, u32[]{:S(2)}) copy-start(s32[1,2]{1,0:T(1,128)} %rim_ref.1) | copy-start | bytes 28
  122.0 31.4 %copy-start.4 = (s32[24,8]{0,1:T(8,128)S(1)}, s32[24,8]{0,1:T(8,128)}, u32[]{:S(2)}) copy-start(s32[24,8]{0,1:T(8,128)} %param.11) | copy-start | bytes 2308
  122.0 31.5 %copy-start.1 = (bf16[1536,512]{1,0:T(8,128)(2,1)S(1)}, bf16[1536,512]{1,0:T(8,128)(2,1)}, u32[]{:S(2)}) copy-start(bf16[1536,512]{1,0:T(8,128)(2,1)} %jac_ref.1) | copy-start | bytes 4718596

commit v3 on v2

--- a/solution.py
+++ b/solution.py
@@ -145,7 +145,7 @@
             newton_step(a.at[i], z.at[i])
 
     def unsettled(state):
-        return jnp.logical_and(state[0] < most, state[1] > 1e-7)
+        return jnp.logical_and(state[0] < most, state[1] > 3e-5)
 
     def again(state):
         for i in range(count):
@@ -154,7 +154,7 @@
 
     left = lax.while_loop(unsettled, again, (jnp.int32(fixed), residual(a, count)))[1]
 
-    @pl.when(left > 1e-7)
+    @pl.when(left > 3e-5)
     def _():
         def direct(i, _):
             chol_inv(first.at[i], z.at[i], wide)
@@ -275,7 +275,7 @@
         copy.wait_recv()
 
 
-def give_over_space(ph, chunk, g1, g2, out):
+def give_over_space(ph, chunk, g1, g2, out, beside=None):
     copies = []
     for half in (0, 1):
         mine = rows_of(ph.own(half, False), 8)
@@ -292,6 +292,8 @@
             _, device = ph.along(half, True, d)
             copies.append(ph.send(g1.at[half], g2.at[half, :, mine, :], device))
         g2[half, :, mine, :] = g1[half]
+    if beside is not None:
+        beside()
     for copy in copies:
         copy.wait_recv()
     mine = rows_of(ph.core, 128)
@@ -316,20 +318,24 @@
 
 
 def first_sum(
-    x_ref, w_ref, om_ref, out_ref, parts_ref, zo_ref,
-    part, bc, bx, by, s1, s2, s3, spread, chunk, g1, g2, got, sends, arrivals, parts, m, zo, wide
+    count_ref, x_ref, volume_ref, om_ref, out_ref, parts_ref, zo_ref,
+    part, bc, bx, by, s1, s2, s3, spread, chunk, g1, g2, got, sends, arrivals, local, parts, m, zo, wide
 ):
     ph = Phases(sends, arrivals)
     ph.greet(ph.peers())
-    weighted = jnp.transpose(x_ref[...]).astype(F32) * w_ref[...]
-    put_halves(part, 0, mm2(weighted, x_ref[...]))
+    used = count_ref[0] * BLOCK
+    local[...] = jnp.where(iota(x_ref.shape, 0) < used, x_ref[...], 0)
+    total = x_ref.shape[0] * lax.axis_size("space")
+    weight = jnp.where(iota(volume_ref.shape, 1) < used, volume_ref[...], 0.0) / total
+    weighted = jnp.transpose(local[...]).astype(F32) * weight
+    put_halves(part, 0, mm2(weighted, local[...]))
     ph.met(10)
     quarter = parts.shape[1]
 
     def give_rows(d):
         there = ph.other(d)
         rows = quarter_rows(lax.rem(there, 4), quarter)
-        return ph.send(x_ref.at[rows, :], parts.at[d - 1], {"snap": there})
+        return ph.send(local.at[rows, :], parts.at[d - 1], {"snap": there})
 
     bulk = [give_rows(2), give_rows(1)]
     om = om_ref[ph.core]
@@ -341,28 +347,73 @@
     bulk.append(give_rows(3))
     for d in range(4):
         chunk[:, d] = spread[d, :, 0]
-    give_over_space(ph, chunk, g1, g2, got)
-    chol_lower(mine, wide)
+    give_over_space(ph, chunk, g1, g2, got, lambda: chol_lower(mine, wide))
     factor_copy = ph.send(mine, mine, {"space": ph.space(ph.x, ph.y, 1 - ph.core)})
     for d in range(4):
         out_ref[d] = whole(got, d)
-    for copy in bulk:
+    parts_ref[0] = local[quarter_rows(ph.place, quarter), :]
+    for d, copy in zip((2, 1, 3), bulk):
         copy.wait_recv()
-    parts_ref[...] = parts[...]
+        parts_ref[d] = parts[d - 1]
     factor_copy.wait_recv()
     zo_ref[...] = zo[...]
     ph.finish()
 
 
-def second_sum(part, out_ref, bc, bx, by, s1, s2, s3, spread, chunk, g1, g2, got, sends, arrivals):
+def gram_factors(g_ref, z, a, first, start, wide):
+    rank = g_ref.shape[1]
+    diagonal = iota((rank, rank), 0) == iota((rank, rank), 1)
+    for d in range(4):
+        g = g_ref[d]
+        pivots = jnp.where(diagonal, g, 0.0)
+        down = lax.rsqrt(jnp.sum(pivots, axis=1, keepdims=True))
+        across = lax.rsqrt(jnp.sum(pivots, axis=0, keepdims=True))
+        a[d] = g * down * across
+        z[d] = jnp.where(diagonal, down, 0.0)
+    factor(a, z, first, start, wide, 4, 3, 8)
+
+
+def second_sum(
+    count_ref, z_ref, x_ref, volume_ref, om_ref, out_ref, sk_ref,
+    part, bc, bx, by, s1, s2, s3, spread, chunk, g1, g2, got, sends, arrivals, base, sketch
+):
     ph = Phases(sends, arrivals)
     ph.greet(ph.peers())
+    rank = om_ref.shape[2]
+    quarter = x_ref.shape[1]
+    for d in range(4):
+        base[lax.rem(ph.other(d), 4)] = mm2r(x_ref[d], z_ref[d], NT).astype(BF16)
+    start = quarter_rows(ph.place, quarter)
+    used = count_ref[0] * BLOCK
+    lanes = iota((1, quarter), 1) + (2 * lax.rem(ph.place, 2) + ph.place // 2) * quarter
+    total = 4 * quarter * lax.axis_size("space")
+    weight = jnp.where(lanes < used, volume_ref[:, start], 0.0) / total
+    mine = sketch.at[ph.place // 2]
+    for pair in (0, 1):
+        low, high = base[2 * pair], base[2 * pair + 1]
+        both = mm(low, om_ref[0, :rank, :]) + mm(high, om_ref[0, rank:, :])
+        mine[:, pair * rank : (pair + 1) * rank] = both.astype(BF16)
+        put_halves(part, pair, mm2(jnp.transpose(low).astype(F32) * weight, high))
+    low, high = mine[:, :rank], mine[:, rank:]
+    put_halves(part, 2, mm2(jnp.transpose(low).astype(F32) * weight, high))
     ph.met(10)
+    far = {"snap": ph.other(2)}
+    piece = quarter // 2
+
+    def give_sketch(i):
+        rows = mine.at[pl.ds(i * piece, piece), :]
+        return ph.send(rows, rows, far)
+
+    bulk = [give_sketch(0)]
     sum_over_space(ph, part, bc, bx, by, s1, s2, s3, spread)
+    bulk.append(give_sketch(1))
     chunk[...] = (spread[0] + spread[1]) + (spread[2] + spread[3])
     give_over_space(ph, chunk, g1, g2, got)
     for d in range(3):
         out_ref[d] = whole(got, d)
+    for copy in bulk:
+        copy.wait_recv()
+    sk_ref[...] = sketch[...].reshape(sk_ref.shape)
     ph.finish()
 
 
@@ -384,31 +435,6 @@
     ]
 
 
-def basis_kernel(place_ref, g_ref, x0, xs, w_ref, om_ref, sk_ref, part_ref, a, z, first, start, wide, base):
-    place = place_ref[0]
-    rank = om_ref.shape[2]
-    diagonal = iota((rank, rank), 0) == iota((rank, rank), 1)
-    for d in range(4):
-        g = g_ref[d]
-        pivots = jnp.where(diagonal, g, 0.0)
-        down = lax.rsqrt(jnp.sum(pivots, axis=1, keepdims=True))
-        across = lax.rsqrt(jnp.sum(pivots, axis=0, keepdims=True))
-        a[d] = g * down * across
-        z[d] = jnp.where(diagonal, down, 0.0)
-    factor(a, z, first, start, wide, 4, 3, 8)
-    for d in range(4):
-        x = x0[...] if d == 0 else xs[d - 1]
-        base[place ^ d] = mm2r(x, z[d], NT).astype(BF16)
-    weight = w_ref[...]
-    for pair in (0, 1):
-        low, high = base[2 * pair], base[2 * pair + 1]
-        sketch = mm(low, om_ref[0, :rank, :]) + mm(high, om_ref[0, rank:, :])
-        sk_ref[:, pair * rank : (pair + 1) * rank] = sketch.astype(BF16)
-        put_halves(part_ref, pair, mm2(jnp.transpose(low).astype(F32) * weight, high))
-    low, high = sk_ref[:, :rank], sk_ref[:, rank:]
-    put_halves(part_ref, 2, mm2(jnp.transpose(low).astype(F32) * weight, high))
-
-
 def near_identity(z, om, cross, a, t):
     rank = cross.shape[0]
     qa = mm2(z, om[:rank], NT)
@@ -417,7 +443,7 @@
     a[...] = eye(rank) + t[...] + jnp.transpose(t[...])
 
 
-def final_kernel(c_ref, om_ref, zo_ref, sk_ref, out_ref, a, z, first, start, t, wide):
+def merge_factors(c_ref, om_ref, zo_ref, out_ref, a, z, first, start, t, wide):
     rank = om_ref.shape[2]
     for pair in (0, 1):
         near_identity(zo_ref[0], om_ref[0], c_ref[pair], a.at[pair], t.at[pair])
@@ -426,61 +452,54 @@
     cross = mm3(mm3(z[0], c_ref[2]), z[1], NT)
     near_identity(zo_ref[1], om_ref[1], cross, a.at[2], t.at[0])
     z[2] = zo_ref[1]
-    factor(
-        a.at[pl.ds(2, 1)], z.at[pl.ds(2, 1)], first, start, wide, 1, 3, 8
-    )
+    factor(a.at[pl.ds(2, 1)], z.at[pl.ds(2, 1)], first, start, wide, 1, 3, 8)
     last = z[2]
     for pair in (0, 1):
         u = mm2r(om_ref[1, pair * rank : (pair + 1) * rank, :], last, NT)
-        t[pair] = mm3(jnp.transpose(z[pair]), u)
-    left, right = split(t[0]), split(t[1])
-    low, high = sk_ref[:, :rank], sk_ref[:, rank:]
-    final = (mm(low, left[0]) + mm(high, right[0])) + (mm(low, left[1]) + mm(high, right[1]))
-    out_ref[...] = final.astype(BF16)
-
-
-def spread_kernel(rim_ref, own_ref, base_ref, rims_ref, base, rim_out, rim_in, sends, arrivals):
+        out_ref[pair * rank : (pair + 1) * rank, :] = mm3(jnp.transpose(z[pair]), u)
+
+
+def spread_kernel(
+    rim_ref, sk_ref, mix_ref, base_ref, rims_ref, own, base, rim_out, rim_in, sends, arrivals
+):
     ph = Phases(sends, arrivals)
-    near, far = ph.other(1), ph.other(2)
     me, n = lax.axis_index("space"), lax.axis_size("space")
-    before, after = {"space": lax.rem(me + n - 1, n)}, {"space": lax.rem(me + 1, n)}
-    ph.greet([{"snap": near}, {"snap": far}, before, after])
-    quarter = own_ref.shape[0] // BLOCK
-    pieces = 3
-    size = quarter // pieces
-
-    def rows(place, piece):
-        return pl.ds((2 * lax.rem(place, 2) + place // 2) * quarter + piece * size, size)
-
-    own = own_ref[...].reshape(quarter, BLOCK, own_ref.shape[1])
+    near = ph.other(1)
+    before, after = lax.rem(me + n - 1, n), lax.rem(me + 1, n)
+    targets = [{"space": before}, {"space": after}]
+    targets += [{"space": before, "snap": near}, {"space": after, "snap": near}]
+    ph.greet([{"snap": near}] + targets)
+    high, low = split(mix_ref[...])
+    half = base.shape[0] // 2
+    upper = lax.rem(ph.place, 2)
+    pieces = 4
+    size = half // pieces
     for piece in range(pieces):
-        base[rows(ph.place, piece)] = own[piece * size : (piece + 1) * size]
-    ph.met(4)
-    across, relayed = [], []
-    for piece in range(pieces):
-        mine = base.at[rows(ph.place, piece)]
-        across.append(ph.send(mine, mine, {"snap": far}))
-    for piece in range(pieces):
-        mine = base.at[rows(ph.place, piece)]
-        relayed.append(ph.send(mine, mine, {"snap": near}))
-    for piece in range(pieces):
-        across[piece].wait_recv()
-        theirs = base.at[rows(lax.rem(far, 4), piece)]
-        relayed.append(ph.send(theirs, theirs, {"snap": near}))
-    for copy in relayed:
-        copy.wait_recv()
+        rows = slice(piece * size * BLOCK, (piece + 1) * size * BLOCK)
+        sk = sk_ref[rows, :]
+        found = (mm(sk, high) + mm(sk, low)).astype(BF16)
+        own[piece * size : (piece + 1) * size] = found.reshape(size, *own.shape[1:])
+    ph.met(5)
+    mine = base.at[pl.ds(upper * half, half)]
+    copy = ph.send(own, mine, {"snap": near})
     for side in (0, 1):
-        rim_out[side] = base[rim_ref[0, side]]
-
+        where = rim_ref[0, side] - upper * half
+        block = own[jnp.clip(where, 0, half - 1)]
+        inside = jnp.logical_and(where >= 0, where < half)
+        rim_out[side] = jnp.where(inside, block, jnp.zeros_like(block))
     swaps = [
-        ph.send(rim_out.at[0], rim_in.at[1], before),
-        ph.send(rim_out.at[1], rim_in.at[0], after),
+        ph.send(rim_out.at[0], rim_in.at[1, 0], targets[0]),
+        ph.send(rim_out.at[1], rim_in.at[0, 0], targets[1]),
+        ph.send(rim_out.at[0], rim_in.at[1, 1], targets[2]),
+        ph.send(rim_out.at[1], rim_in.at[0, 1], targets[3]),
     ]
+    base[pl.ds(upper * half, half)] = own[...]
+    for swap in swaps:
+        swap.wait_recv()
+    rims_ref[:BLOCK, :] = jnp.where(me > 0, rim_in[0, 0] + rim_in[0, 1], 0)
+    rims_ref[BLOCK:, :] = jnp.where(me < n - 1, rim_in[1, 0] + rim_in[1, 1], 0)
+    copy.wait_recv()
     base_ref[...] = base[...].reshape(base_ref.shape)
-    for copy in swaps:
-        copy.wait_recv()
-    rims_ref[:BLOCK, :] = jnp.where(me > 0, rim_in[0], 0)
-    rims_ref[BLOCK:, :] = jnp.where(me < n - 1, rim_in[1], 0)
     ph.finish()
 
 
@@ -523,84 +542,81 @@
 def on_device(snapshots, cell_volume, counts, rim_rows, jac_cols, jacobian, omega):
     rows, rank = snapshots.shape
     blocks, quarter = rows // BLOCK, rows // 4
-    total = rows * lax.axis_size("space")
-    valid = lax.broadcasted_iota(jnp.int32, (blocks, BLOCK), 0).reshape(rows) < counts[0]
-    weight = jnp.where(valid, cell_volume / total, 0.0).reshape(1, rows)
-    local = jnp.where(valid[:, None], snapshots, 0)
-    place = lax.axis_index("snap") % 4
-    start = (2 * (place % 2) + place // 2) * quarter
+    volume = cell_volume.reshape(1, rows)
     square = (rank, rank)
     wide = pltpu.VMEM((rank // 2, rank), F32)
 
     def squares(n):
         return pltpu.VMEM((n, rank, rank), F32)
 
-    grams, others, starts = call(
+    grams, parts, starts = call(
         first_sum,
         [
             jax.ShapeDtypeStruct((4, rank, rank), F32),
-            jax.ShapeDtypeStruct((3, quarter, rank), BF16),
+            jax.ShapeDtypeStruct((4, quarter, rank), BF16),
             jax.ShapeDtypeStruct((2, rank, rank), F32),
         ],
-        [VM] * 3,
+        [SM] + [VM] * 3,
         [pltpu.VMEM((2, 1, rank, rank // 2), F32)]
         + sum_scratch(1, 4, 33)
-        + [pltpu.VMEM((3, quarter, rank), BF16), pltpu.VMEM(square, F32), squares(2), wide],
+        + [
+            pltpu.VMEM((rows, rank), BF16),
+            pltpu.VMEM((3, quarter, rank), BF16),
+            pltpu.VMEM(square, F32),
+            squares(2),
+            wide,
+        ],
         "first_sum",
         collective_id=0,
         has_side_effects=True,
-    )(local, weight, omega)
-    sketch, cross = call(
-        basis_kernel,
+    )(counts, snapshots, volume, omega)
+    factors = call(
+        gram_factors,
+        jax.ShapeDtypeStruct((4, rank, rank), F32),
+        [VM],
+        [squares(4)] * 3 + [wide],
+        "gram_factors",
+    )(grams)
+    cross, sketch = call(
+        second_sum,
         [
-            jax.ShapeDtypeStruct((quarter, 2 * rank), BF16),
-            jax.ShapeDtypeStruct((2, 3, rank, rank // 2), F32),
+            jax.ShapeDtypeStruct((3, rank, rank), F32),
+            jax.ShapeDtypeStruct((2 * quarter, 2 * rank), BF16),
         ],
-        [SM] + [VM] * 5,
-        [squares(4)] * 4 + [wide, pltpu.VMEM((4, quarter, rank), BF16)],
-        "bases",
-    )(
-        place.reshape(1),
-        grams,
-        lax.dynamic_slice_in_dim(local, start, quarter, 0),
-        others,
-        lax.dynamic_slice_in_dim(weight, start, quarter, 1),
-        omega,
-    )
-    cross = call(
-        second_sum,
-        jax.ShapeDtypeStruct((3, rank, rank), F32),
-        [VM],
-        sum_scratch(3, 3),
+        [SM] + [VM] * 4,
+        [pltpu.VMEM((2, 3, rank, rank // 2), F32)]
+        + sum_scratch(3, 3, 31)
+        + [pltpu.VMEM((4, quarter, rank), BF16), pltpu.VMEM((2, quarter, 2 * rank), BF16)],
         "second_sum",
         collective_id=1,
         has_side_effects=True,
-    )(cross)
-    final = call(
-        final_kernel,
-        jax.ShapeDtypeStruct((quarter, rank), BF16),
-        [VM] * 4,
+    )(counts, factors, parts, volume, omega)
+    mix = call(
+        merge_factors,
+        jax.ShapeDtypeStruct((2 * rank, rank), F32),
+        [VM] * 3,
         [squares(3), squares(3), squares(2), squares(2), squares(2), wide],
-        "final_rows",
-    )(cross, omega, starts, sketch)
+        "merge_factors",
+    )(cross, omega, starts)
     full, rims = call(
         spread_kernel,
         [
             jax.ShapeDtypeStruct((rows, rank), BF16),
             jax.ShapeDtypeStruct((2 * BLOCK, rank), BF16),
         ],
-        [SM, VM],
+        [SM, VM, VM],
         [
+            pltpu.VMEM((blocks // 2, BLOCK, rank), BF16),
             pltpu.VMEM((blocks, BLOCK, rank), BF16),
             pltpu.VMEM((2, BLOCK, rank), BF16),
-            pltpu.VMEM((2, BLOCK, rank), BF16),
-            pltpu.SemaphoreType.DMA((11,)),
-            pltpu.SemaphoreType.DMA((11,)),
+            pltpu.VMEM((2, 2, BLOCK, rank), BF16),
+            pltpu.SemaphoreType.DMA((5,)),
+            pltpu.SemaphoreType.DMA((5,)),
         ],
         "spread_rows",
         collective_id=2,
         has_side_effects=True,
-    )(rim_rows, final)
+    )(rim_rows, sketch, mix)
     basis, product = call(
         product_kernel,
         [jax.ShapeDtypeStruct((rows, rank), BF16)] * 2,

time: 158 us -> 147 us (0.930)
  Pallas kernels: 155 us -> 143 us
  local copies, waits for them, and re-layouts: 0.3 us -> 2.97 us
    pallas_call x1, Pallas kernels: 37.5 us -> 32.9 us  [on_device(): call(first_sum, [jax.ShapeDtypeStruct((4, rank, rank), F32), jax.ShapeDty...]
    pallas_call x1, Pallas kernels: 21.2 us -> 17 us  [on_device(): call(spread_kernel, [jax.ShapeDtypeStruct((rows, rank), BF16), jax.ShapeD...]
    pallas_call x3, Pallas kernels: 91.6 us -> 88.4 us  [the longest x1 53.1 us: on_device(): call(gram_factors, jax.ShapeDtypeStruct((4, rank, rank), F32), [VM], [squ...]
    unnamed x11 -> x13, local copies, waits for them, and re-layouts: 0.1 us -> 2.27 us
where the time goes in v3:
time: 147 us
  Pallas kernels  143 us (97%)
  local copies, waits for them, and re-layouts  2.97 us (2%)
    pallas_call x1, Pallas kernels, on_device(): call(gram_factors, jax.ShapeDtypeStruct((4, rank, rank), F32), [VM], [squ...  53.1 us
    pallas_call x1, Pallas kernels, on_device(): call(first_sum, [jax.ShapeDtypeStruct((4, rank, rank), F32), jax.ShapeDty...  32.9 us
    pallas_call x1, Pallas kernels, on_device(): call(second_sum, [jax.ShapeDtypeStruct((3, rank, rank), F32), jax.ShapeDt...  27.1 us
    pallas_call x1, Pallas kernels, on_device(): call(spread_kernel, [jax.ShapeDtypeStruct((rows, rank), BF16), jax.ShapeD...  17 us
    pallas_call x1, Pallas kernels, on_device(): call(merge_factors, jax.ShapeDtypeStruct((2 * rank, rank), F32), [VM] * 3...  8.15 us
    pallas_call x1, Pallas kernels, on_device(): call(product_kernel, [jax.ShapeDtypeStruct((rows, rank), BF16)] * 2, [SM,...  4.37 us

profile of v3, /device:TPU:128, one launch (start us, length us, event | category | flops | bytes accessed | tf_op | source)
XLA Modules:
  0.0 147.0 jit_solution(7889689960762640862)
XLA Ops:
  1.3 0.7 reshape.7.volume_ref
  2.0 0.0 copy-start
  2.0 1.0 copy-done
  3.0 0.0 copy-start.3
  3.0 1.1 copy-done.3
  4.2 0.0 copy-start.1
  4.2 32.9 %first_sum.1 = (f32[4,256,256]{2,1,0:T(8,128)S(1)}, bf16[4,384,256]{2,1,0:T(8,128)(2,1)S(1)}, f32[2,256,256]{2,1,0:T(8,128)S(1)}) custom-call(s32[1]{0:T(128)S(6)} %copy.10.count_ref, bf16[1536,256]{1,0:T(8,128)(2,1)S(1)} %copy-done.3, f32[1,1536]{1,0:T(1,128)S(1)} %reshape.7.volume_ref, bf16[2,512,256]{2,1,0:T(8,128)(2,1)S(1)} %copy-done), custom_call_target="tpu_custom_call" | custom-call | tf_op jit(solution)/shard_map/first_sum/pallas_call | solution.py:552
  37.1 53.1 %gram_factors.1.z_ref = f32[4,256,256]{2,1,0:T(8,128)S(1)} custom-call(f32[4,256,256]{2,1,0:T(8,128)S(1)} %get-tuple-element.9.g_ref), custom_call_target="tpu_custom_call" | custom-call | tf_op jit(solution)/shard_map/gram_factors/pallas_call | solution.py:573
  90.2 0.0 copy-done.1
  90.2 27.1 %second_sum.1 = (f32[3,256,256]{2,1,0:T(8,128)S(1)}, bf16[768,512]{1,0:T(8,128)(2,1)S(1)}) custom-call(s32[1]{0:T(128)S(6)} %copy.10.count_ref, f32[4,256,256]{2,1,0:T(8,128)S(1)} %gram_factors.1.z_ref, bf16[4,384,256]{2,1,0:T(8,128)(2,1)S(1)} %get-tuple-element.10.x_ref, f32[1,1536]{1,0:T(1,128)S(1)} %reshape.7.volume_ref, bf16[2,512,256]{2,1,0:T(8,128)(2,1)S(1)} %copy-done.1), custom_call_target="tpu_custom_call" | custom-call | tf_op jit(solution)/shard_map/second_sum/pallas_call | solution.py:580
  117.3 0.0 copy-start.4
  117.4 0.0 copy-start.5
  117.4 0.0 copy-start.2
  117.4 8.1 %merge_factors.1.mix_ref = f32[512,256]{1,0:T(8,128)S(1)} custom-call(f32[3,256,256]{2,1,0:T(8,128)S(1)} %get-tuple-element.12.c_ref, bf16[2,512,256]{2,1,0:T(8,128)(2,1)S(1)} %copy-done.1, f32[2,256,256]{2,1,0:T(8,128)S(1)} %get-tuple-element.13.zo_ref), custom_call_target="tpu_custom_call" | custom-call | tf_op jit(solution)/shard_map/merge_factors/pallas_call | solution.py:594
  125.5 0.0 copy-done.4
  125.5 17.0 %spread_rows.1 = (bf16[1536,256]{1,0:T(8,128)(2,1)S(1)}, bf16[128,256]{1,0:T(8,128)(2,1)S(1)}) custom-call(s32[1,2]{1,0:T(1,128)S(1)} %copy-done.4, bf16[768,512]{1,0:T(8,128)(2,1)S(1)} %get-tuple-element.11.sk_ref, f32[512,256]{1,0:T(8,128)S(1)} %merge_factors.1.mix_ref), custom_call_target="tpu_custom_call" | custom-call | tf_op jit(solution)/shard_map/spread_rows/pallas_call | solution.py:601
  142.5 0.0 copy-done.5
  142.5 0.1 copy.9.cols_ref
  142.6 0.0 copy-done.2
  142.6 4.4 %jac_product.1 = (bf16[1536,256]{1,0:T(8,128)(2,1)}, bf16[1536,256]{1,0:T(8,128)(2,1)}) custom-call(s32[24,8]{1,0:T(8,128)S(1)} %copy.9.cols_ref, s32[1]{0:T(128)S(6)} %copy.10.count_ref, bf16[1536,256]{1,0:T(8,128)(2,1)S(1)} %get-tuple-element.14.full_ref, bf16[128,256]{1,0:T(8,128)(2,1)S(1)} %get-tuple-element.15.rims_ref, bf16[1536,512]{1,0:T(8,128)(2,1)S(1)} %copy-done.2), custom_call_target="tpu_custom_call" | custom-call | tf_op jit(solution)/shard_map/jac_product/pallas_call | solution.py:620
Async XLA Ops:
  2.0 1.0 copy-start
  3.0 1.1 copy-start.3
  4.2 86.1 %copy-start.1 = (bf16[2,512,256]{2,1,0:T(8,128)(2,1)S(1)}, bf16[2,512,256]{2,1,0:T(8,128)(2,1)}, u32[]{:S(2)}) copy-start(bf16[2,512,256]{2,1,0:T(8,128)(2,1)} %om_ref.5) | copy-start | bytes 1572868
  117.3 8.2 %copy-start.4 = (s32[1,2]{1,0:T(1,128)S(1)}, s32[1,2]{1,0:T(1,128)}, u32[]{:S(2)}) copy-start(s32[1,2]{1,0:T(1,128)} %rim_ref.1) | copy-start | bytes 28
  117.4 25.2 %copy-start.5 = (s32[24,8]{0,1:T(8,128)S(1)}, s32[24,8]{0,1:T(8,128)}, u32[]{:S(2)}) copy-start(s32[24,8]{0,1:T(8,128)} %param.11) | copy-start | bytes 2308
  117.4 25.3 %copy-start.2 = (bf16[1536,512]{1,0:T(8,128)(2,1)S(1)}, bf16[1536,512]{1,0:T(8,128)(2,1)}, u32[]{:S(2)}) copy-start(bf16[1536,512]{1,0:T(8,128)(2,1)} %jac_ref.1) | copy-start | bytes 4718596

commit v4 on v3

--- a/solution.py
+++ b/solution.py
@@ -117,10 +117,18 @@
     return mm(a, high, dims) + mm(a, low, dims)
 
 
-def newton_step(a_ref, z_ref):
+def newton_step(a_ref, z_ref, rough=False):
     a = a_ref[...]
     row, col = iota(a.shape, 0), iota(a.shape, 1)
-    h = split(jnp.where(row > col, -a, jnp.where(row == col, 1.5 - 0.5 * a, 0.0)))
+    h = jnp.where(row > col, -a, jnp.where(row == col, 1.5 - 0.5 * a, 0.0))
+    if rough:
+        h = h.astype(BF16)
+        t = mm2r(h, a)
+        z = mm2r(h, z_ref[...])
+        a_ref[...] = mm2(t, h, NT)
+        z_ref[...] = z
+        return
+    h = split(h)
     t = mm3s(h, split(a))
     z = mm3s(h, split(z_ref[...]))
     a_ref[...] = mm3s(split(t), h, NT)
@@ -140,9 +148,9 @@
     for i in range(count):
         first[i] = a[i]
         start[i] = z[i]
-    for _ in range(fixed):
+    for step in range(fixed):
         for i in range(count):
-            newton_step(a.at[i], z.at[i])
+            newton_step(a.at[i], z.at[i], step < 2)
 
     def unsettled(state):
         return jnp.logical_and(state[0] < most, state[1] > 3e-5)
@@ -318,15 +326,24 @@
 
 
 def first_sum(
-    count_ref, x_ref, volume_ref, om_ref, out_ref, parts_ref, zo_ref,
-    part, bc, bx, by, s1, s2, s3, spread, chunk, g1, g2, got, sends, arrivals, local, parts, m, zo, wide
+    count_ref, x_ref, volume_ref, om_ref, out_ref, parts_ref, zo_ref, weight_ref,
+    part, bc, bx, by, s1, s2, s3, spread, chunk, g1, g2, got, sends, arrivals,
+    raw, om_local, loads, local, parts, m, zo, wide
 ):
     ph = Phases(sends, arrivals)
+    load = pltpu.make_async_copy(x_ref, raw, loads.at[0])
+    load.start()
+    om_load = pltpu.make_async_copy(om_ref.at[ph.core], om_local, loads.at[1])
+    om_load.start()
     ph.greet(ph.peers())
     used = count_ref[0] * BLOCK
-    local[...] = jnp.where(iota(x_ref.shape, 0) < used, x_ref[...], 0)
-    total = x_ref.shape[0] * lax.axis_size("space")
-    weight = jnp.where(iota(volume_ref.shape, 1) < used, volume_ref[...], 0.0) / total
+    rows = raw.shape[0]
+    total = rows * lax.axis_size("space")
+    volume = volume_ref[...].reshape(1, rows)
+    weight = jnp.where(iota((1, rows), 1) < used, volume, 0.0) / total
+    weight_ref[...] = weight
+    load.wait()
+    local[...] = jnp.where(iota(raw.shape, 0) < used, raw[...], 0)
     weighted = jnp.transpose(local[...]).astype(F32) * weight
     put_halves(part, 0, mm2(weighted, local[...]))
     ph.met(10)
@@ -338,7 +355,8 @@
         return ph.send(local.at[rows, :], parts.at[d - 1], {"snap": there})
 
     bulk = [give_rows(2), give_rows(1)]
-    om = om_ref[ph.core]
+    om_load.wait()
+    om = om_local[...]
     m[...] = mm(om, om, TN)
     mine = zo.at[ph.core]
     sum_over_space(
@@ -374,7 +392,7 @@
 
 
 def second_sum(
-    count_ref, z_ref, x_ref, volume_ref, om_ref, out_ref, sk_ref,
+    z_ref, x_ref, weight_ref, om_ref, zo_ref, out_ref, sk_ref, q_ref,
     part, bc, bx, by, s1, s2, s3, spread, chunk, g1, g2, got, sends, arrivals, base, sketch
 ):
     ph = Phases(sends, arrivals)
@@ -383,12 +401,8 @@
     quarter = x_ref.shape[1]
     for d in range(4):
         base[lax.rem(ph.other(d), 4)] = mm2r(x_ref[d], z_ref[d], NT).astype(BF16)
-    start = quarter_rows(ph.place, quarter)
-    used = count_ref[0] * BLOCK
-    lanes = iota((1, quarter), 1) + (2 * lax.rem(ph.place, 2) + ph.place // 2) * quarter
-    total = 4 * quarter * lax.axis_size("space")
-    weight = jnp.where(lanes < used, volume_ref[:, start], 0.0) / total
-    mine = sketch.at[ph.place // 2]
+    weight = weight_ref[:, quarter_rows(ph.place, quarter)]
+    mine = sketch.at[2 * lax.rem(ph.place, 2) + ph.place // 2]
     for pair in (0, 1):
         low, high = base[2 * pair], base[2 * pair + 1]
         both = mm(low, om_ref[0, :rank, :]) + mm(high, om_ref[0, rank:, :])
@@ -397,23 +411,29 @@
     low, high = mine[:, :rank], mine[:, rank:]
     put_halves(part, 2, mm2(jnp.transpose(low).astype(F32) * weight, high))
     ph.met(10)
-    far = {"snap": ph.other(2)}
     piece = quarter // 2
 
-    def give_sketch(i):
+    def give_sketch(d, i):
         rows = mine.at[pl.ds(i * piece, piece), :]
-        return ph.send(rows, rows, far)
-
-    bulk = [give_sketch(0)]
-    sum_over_space(ph, part, bc, bx, by, s1, s2, s3, spread)
-    bulk.append(give_sketch(1))
+        return ph.send(rows, rows, {"snap": ph.other(d)})
+
+    def omega_products():
+        for level in (0, 1):
+            q_ref[level, 0] = mm2(zo_ref[level], om_ref[level, :rank, :], NT)
+            q_ref[level, 1] = mm2r(om_ref[level, rank:, :], zo_ref[level], NT)
+
+    bulk = [give_sketch(2, 0), give_sketch(1, 0)]
+    sum_over_space(ph, part, bc, bx, by, s1, s2, s3, spread, omega_products)
+    bulk += [give_sketch(2, 1), give_sketch(1, 1)]
     chunk[...] = (spread[0] + spread[1]) + (spread[2] + spread[3])
     give_over_space(ph, chunk, g1, g2, got)
     for d in range(3):
         out_ref[d] = whole(got, d)
     for copy in bulk:
         copy.wait_recv()
-    sk_ref[...] = sketch[...].reshape(sk_ref.shape)
+    for i, d in enumerate((0, 2, 1)):
+        there = lax.rem(ph.other(d), 4)
+        sk_ref[i] = sketch[2 * lax.rem(there, 2) + there // 2]
     ph.finish()
 
 
@@ -435,22 +455,20 @@
     ]
 
 
-def near_identity(z, om, cross, a, t):
-    rank = cross.shape[0]
-    qa = mm2(z, om[:rank], NT)
-    qb = mm2r(om[rank:], z, NT)
+def near_identity(qa, cross, qb, a, t):
     t[...] = mm3(qa, mm3(cross, qb))
-    a[...] = eye(rank) + t[...] + jnp.transpose(t[...])
-
-
-def merge_factors(c_ref, om_ref, zo_ref, out_ref, a, z, first, start, t, wide):
+    a[...] = eye(cross.shape[0]) + t[...] + jnp.transpose(t[...])
+
+
+def merge_factors(c_ref, om_ref, zo_ref, q_ref, out_ref, a, z, first, start, t, wide):
     rank = om_ref.shape[2]
     for pair in (0, 1):
-        near_identity(zo_ref[0], om_ref[0], c_ref[pair], a.at[pair], t.at[pair])
+        near_identity(q_ref[0, 0], c_ref[pair], q_ref[0, 1], a.at[pair], t.at[pair])
         z[pair] = zo_ref[0]
     factor(a, z, first, start, wide, 2, 3, 8)
-    cross = mm3(mm3(z[0], c_ref[2]), z[1], NT)
-    near_identity(zo_ref[1], om_ref[1], cross, a.at[2], t.at[0])
+    t[0] = mm3(q_ref[1, 0], z[0])
+    t[1] = mm3(jnp.transpose(z[1]), q_ref[1, 1])
+    near_identity(t[0], c_ref[2], t[1], a.at[2], t.at[0])
     z[2] = zo_ref[1]
     factor(a.at[pl.ds(2, 1)], z.at[pl.ds(2, 1)], first, start, wide, 1, 3, 8)
     last = z[2]
@@ -471,17 +489,23 @@
     ph.greet([{"snap": near}] + targets)
     high, low = split(mix_ref[...])
     half = base.shape[0] // 2
+    quarter = half // 2
     upper = lax.rem(ph.place, 2)
-    pieces = 4
-    size = half // pieces
-    for piece in range(pieces):
-        rows = slice(piece * size * BLOCK, (piece + 1) * size * BLOCK)
-        sk = sk_ref[rows, :]
+    second = ph.place // 2
+
+    def rows_from(sk):
         found = (mm(sk, high) + mm(sk, low)).astype(BF16)
-        own[piece * size : (piece + 1) * size] = found.reshape(size, *own.shape[1:])
+        return found.reshape(quarter, *own.shape[1:])
+
+    own[pl.ds(second * quarter, quarter)] = rows_from(sk_ref[0])
+    own[pl.ds((1 - second) * quarter, quarter)] = rows_from(sk_ref[1])
     ph.met(5)
-    mine = base.at[pl.ds(upper * half, half)]
-    copy = ph.send(own, mine, {"snap": near})
+    sent = upper * half + (1 - second) * quarter
+    copy = ph.send(
+        own.at[pl.ds((1 - second) * quarter, quarter)],
+        base.at[pl.ds(sent, quarter)],
+        {"snap": near},
+    )
     for side in (0, 1):
         where = rim_ref[0, side] - upper * half
         block = own[jnp.clip(where, 0, half - 1)]
@@ -494,6 +518,7 @@
         ph.send(rim_out.at[1], rim_in.at[0, 1], targets[3]),
     ]
     base[pl.ds(upper * half, half)] = own[...]
+    base[pl.ds((1 - upper) * half + second * quarter, quarter)] = rows_from(sk_ref[2])
     for swap in swaps:
         swap.wait_recv()
     rims_ref[:BLOCK, :] = jnp.where(me > 0, rim_in[0, 0] + rim_in[0, 1], 0)
@@ -525,6 +550,7 @@
 
 VM = pl.BlockSpec(memory_space=pltpu.VMEM)
 SM = pl.BlockSpec(memory_space=pltpu.SMEM)
+ANY = pl.BlockSpec(memory_space=pl.ANY)
 
 
 def call(body, outs, ins, scratch, name, **params):
@@ -542,24 +568,27 @@
 def on_device(snapshots, cell_volume, counts, rim_rows, jac_cols, jacobian, omega):
     rows, rank = snapshots.shape
     blocks, quarter = rows // BLOCK, rows // 4
-    volume = cell_volume.reshape(1, rows)
     square = (rank, rank)
     wide = pltpu.VMEM((rank // 2, rank), F32)
 
     def squares(n):
         return pltpu.VMEM((n, rank, rank), F32)
 
-    grams, parts, starts = call(
+    grams, parts, starts, weight = call(
         first_sum,
         [
             jax.ShapeDtypeStruct((4, rank, rank), F32),
             jax.ShapeDtypeStruct((4, quarter, rank), BF16),
             jax.ShapeDtypeStruct((2, rank, rank), F32),
+            jax.ShapeDtypeStruct((1, rows), F32),
         ],
-        [SM] + [VM] * 3,
+        [SM, ANY, VM, ANY],
         [pltpu.VMEM((2, 1, rank, rank // 2), F32)]
         + sum_scratch(1, 4, 33)
         + [
+            pltpu.VMEM((rows, rank), BF16),
+            pltpu.VMEM((2 * rank, rank), BF16),
+            pltpu.SemaphoreType.DMA((2,)),
             pltpu.VMEM((rows, rank), BF16),
             pltpu.VMEM((3, quarter, rank), BF16),
             pltpu.VMEM(square, F32),
@@ -569,7 +598,7 @@
         "first_sum",
         collective_id=0,
         has_side_effects=True,
-    )(counts, snapshots, volume, omega)
+    )(counts, snapshots, cell_volume, omega)
     factors = call(
         gram_factors,
         jax.ShapeDtypeStruct((4, rank, rank), F32),
@@ -577,27 +606,28 @@
         [squares(4)] * 3 + [wide],
         "gram_factors",
     )(grams)
-    cross, sketch = call(
+    cross, sketch, products = call(
         second_sum,
         [
             jax.ShapeDtypeStruct((3, rank, rank), F32),
-            jax.ShapeDtypeStruct((2 * quarter, 2 * rank), BF16),
+            jax.ShapeDtypeStruct((3, quarter, 2 * rank), BF16),
+            jax.ShapeDtypeStruct((2, 2, rank, rank), F32),
         ],
-        [SM] + [VM] * 4,
+        [VM] * 5,
         [pltpu.VMEM((2, 3, rank, rank // 2), F32)]
-        + sum_scratch(3, 3, 31)
-        + [pltpu.VMEM((4, quarter, rank), BF16), pltpu.VMEM((2, quarter, 2 * rank), BF16)],
+        + sum_scratch(3, 3, 33)
+        + [pltpu.VMEM((4, quarter, rank), BF16), pltpu.VMEM((4, quarter, 2 * rank), BF16)],
         "second_sum",
         collective_id=1,
         has_side_effects=True,
-    )(counts, factors, parts, volume, omega)
+    )(factors, parts, weight, omega, starts)
     mix = call(
         merge_factors,
         jax.ShapeDtypeStruct((2 * rank, rank), F32),
-        [VM] * 3,
+        [VM] * 4,
         [squares(3), squares(3), squares(2), squares(2), squares(2), wide],
         "merge_factors",
-    )(cross, omega, starts)
+    )(cross, omega, starts, products)
     full, rims = call(
         spread_kernel,
         [

time: 147 us -> 141 us (0.959)
  Pallas kernels: 143 us -> 136 us
    pallas_call x1, Pallas kernels: 17 us -> 12.9 us  [on_device(): call(spread_kernel, [jax.ShapeDtypeStruct((rows, rank), BF16), jax.ShapeD...]
    pallas_call x1, Pallas kernels: 8.15 us -> 6.53 us  [on_device(): call(merge_factors, jax.ShapeDtypeStruct((2 * rank, rank), F32), [VM] * 4...]
    unnamed x13 -> x15, local copies, waits for them, and re-layouts: 2.27 us -> 2.96 us
where the time goes in v4:
time: 141 us
  Pallas kernels  136 us (96%)
  local copies, waits for them, and re-layouts  2.96 us (2%)
    pallas_call x1, Pallas kernels, on_device(): call(gram_factors, jax.ShapeDtypeStruct((4, rank, rank), F32), [VM], [squ...  52.2 us
    pallas_call x1, Pallas kernels, on_device(): call(first_sum, [jax.ShapeDtypeStruct((4, rank, rank), F32), jax.ShapeDty...  33 us
    pallas_call x1, Pallas kernels, on_device(): call(second_sum, [jax.ShapeDtypeStruct((3, rank, rank), F32), jax.ShapeDt...  27.3 us
    pallas_call x1, Pallas kernels, on_device(): call(spread_kernel, [jax.ShapeDtypeStruct((rows, rank), BF16), jax.ShapeD...  12.9 us
    pallas_call x1, Pallas kernels, on_device(): call(merge_factors, jax.ShapeDtypeStruct((2 * rank, rank), F32), [VM] * 4...  6.53 us
    pallas_call x1, Pallas kernels, on_device(): call(product_kernel, [jax.ShapeDtypeStruct((rows, rank), BF16)] * 2, [SM,...  4.37 us
    unnamed x15, local copies, waits for them, and re-layouts  2.96 us

profile of v4, /device:TPU:128, one launch (start us, length us, event | category | flops | bytes accessed | tf_op | source)
XLA Modules:
  0.0 140.6 jit_solution(9174315851025974902)
XLA Ops:
  1.3 0.0 copy-start
  1.3 1.0 copy-done
  2.3 0.0 copy-start.3
  2.3 1.1 copy-done.3
  3.5 0.0 copy-start.4
  3.5 0.7 copy-done.4
  4.2 0.0 copy-start.1
  4.2 33.0 %first_sum.1 = (f32[4,256,256]{2,1,0:T(8,128)S(1)}, bf16[4,384,256]{2,1,0:T(8,128)(2,1)S(1)}, f32[2,256,256]{2,1,0:T(8,128)S(1)}, f32[1,1536]{1,0:T(1,128)S(1)}) custom-call(s32[1]{0:T(128)S(6)} %copy.10.count_ref, bf16[1536,256]{1,0:T(8,128)(2,1)S(1)} %copy-done.3, f32[1536]{0:T(1024)S(1)} %copy-done.4, bf16[2,512,256]{2,1,0:T(8,128)(2,1)S(1)} %copy-done), custom_call_target="tpu_custom_call" | custom-call | tf_op jit(solution)/shard_map/first_sum/pallas_call | solution.py:577
  37.2 52.2 %gram_factors.1.z_ref = f32[4,256,256]{2,1,0:T(8,128)S(1)} custom-call(f32[4,256,256]{2,1,0:T(8,128)S(1)} %get-tuple-element.11.g_ref), custom_call_target="tpu_custom_call" | custom-call | tf_op jit(solution)/shard_map/gram_factors/pallas_call | solution.py:602
  89.4 0.0 copy-done.1
  89.4 27.3 %second_sum.1 = (f32[3,256,256]{2,1,0:T(8,128)S(1)}, bf16[3,384,512]{2,1,0:T(8,128)(2,1)S(1)}, f32[2,2,256,256]{3,2,1,0:T(8,128)S(1)}) custom-call(f32[4,256,256]{2,1,0:T(8,128)S(1)} %gram_factors.1.z_ref, bf16[4,384,256]{2,1,0:T(8,128)(2,1)S(1)} %get-tuple-element.12.x_ref, f32[1,1536]{1,0:T(1,128)S(1)} %get-tuple-element.13.weight_ref, ...), custom_call_target="tpu_custom_call" | custom-call | tf_op jit(solution)/shard_map/second_sum/pallas_call | solution.py:609
  116.7 0.0 copy-start.5
  116.7 6.5 %merge_factors.1.mix_ref = f32[512,256]{1,0:T(8,128)S(1)} custom-call(f32[3,256,256]{2,1,0:T(8,128)S(1)} %get-tuple-element.16.c_ref, bf16[2,512,256]{2,1,0:T(8,128)(2,1)S(1)} %copy-done.1, f32[2,256,256]{2,1,0:T(8,128)S(1)} %get-tuple-element.14.zo_ref, f32[2,2,256,256]{3,2,1,0:T(8,128)S(1)} %get-tuple-element.17.q_ref), custom_call_target="tpu_custom_call" | custom-call | tf_op jit(solution)/shard_map/merge_factors/pallas_call | solution.py:624
  123.2 0.0 copy-start.6
  123.3 0.0 copy-start.2
  123.3 0.0 copy-done.5
  123.3 12.9 %spread_rows.1 = (bf16[1536,256]{1,0:T(8,128)(2,1)S(1)}, bf16[128,256]{1,0:T(8,128)(2,1)S(1)}) custom-call(s32[1,2]{1,0:T(1,128)S(1)} %copy-done.5, bf16[3,384,512]{2,1,0:T(8,128)(2,1)S(1)} %get-tuple-element.15.sk_ref, f32[512,256]{1,0:T(8,128)S(1)} %merge_factors.1.mix_ref), custom_call_target="tpu_custom_call" | custom-call | tf_op jit(solution)/shard_map/spread_rows/pallas_call | solution.py:631
  136.2 0.0 copy-done.6
  136.2 0.1 copy.9.cols_ref
  136.2 0.0 copy-done.2
  136.2 4.4 %jac_product.1 = (bf16[1536,256]{1,0:T(8,128)(2,1)}, bf16[1536,256]{1,0:T(8,128)(2,1)}) custom-call(s32[24,8]{1,0:T(8,128)S(1)} %copy.9.cols_ref, s32[1]{0:T(128)S(6)} %copy.10.count_ref, bf16[1536,256]{1,0:T(8,128)(2,1)S(1)} %get-tuple-element.18.full_ref, bf16[128,256]{1,0:T(8,128)(2,1)S(1)} %get-tuple-element.19.rims_ref, bf16[1536,512]{1,0:T(8,128)(2,1)S(1)} %copy-done.2), custom_call_target="tpu_custom_call" | custom-call | tf_op jit(solution)/shard_map/jac_product/pallas_call | solution.py:650
Async XLA Ops:
  1.3 1.0 copy-start
  2.3 1.1 copy-start.3
  3.5 0.7 copy-start.4
  4.2 85.3 %copy-start.1 = (bf16[2,512,256]{2,1,0:T(8,128)(2,1)S(1)}, bf16[2,512,256]{2,1,0:T(8,128)(2,1)}, u32[]{:S(2)}) copy-start(bf16[2,512,256]{2,1,0:T(8,128)(2,1)} %om_ref.5) | copy-start | bytes 1572868
  116.7 6.6 %copy-start.5 = (s32[1,2]{1,0:T(1,128)S(1)}, s32[1,2]{1,0:T(1,128)}, u32[]{:S(2)}) copy-start(s32[1,2]{1,0:T(1,128)} %rim_ref.1) | copy-start | bytes 28
  123.2 12.9 %copy-start.6 = (s32[24,8]{0,1:T(8,128)S(1)}, s32[24,8]{0,1:T(8,128)}, u32[]{:S(2)}) copy-start(s32[24,8]{0,1:T(8,128)} %param.11) | copy-start | bytes 2308
  123.3 13.0 %copy-start.2 = (bf16[1536,512]{1,0:T(8,128)(2,1)S(1)}, bf16[1536,512]{1,0:T(8,128)(2,1)}, u32[]{:S(2)}) copy-start(bf16[1536,512]{1,0:T(8,128)(2,1)} %jac_ref.1) | copy-start | bytes 4718596

commit v5 on v4

--- a/solution.py
+++ b/solution.py
@@ -245,21 +245,24 @@
     return pl.ds(pl.multiple_of(place * size, size), size)
 
 
-def sum_over_space(ph, part, bc, bx, by, s1, s2, s3, spread, beside=None):
-    copy = ph.send(
-        part.at[:, :, rows_of(1 - ph.core, 128), :],
-        bc,
-        {"space": ph.space(ph.x, ph.y, 1 - ph.core)},
-    )
-    copy.wait_recv()
+def sum_over_space(ph, part, bc, bx, by, s1, s2, s3, spread, makers, beside, after):
+    twin = {"space": ph.space(ph.x, ph.y, 1 - ph.core)}
+    copies = []
+    for i, make in enumerate(makers):
+        make()
+        which = pl.ds(i, 1)
+        copies.append(
+            ph.send(part.at[:, which, rows_of(1 - ph.core, 128), :], bc.at[:, which], twin)
+        )
+    for copy in copies:
+        copy.wait_recv()
     s1[...] = part[:, :, rows_of(ph.core, 128), :] + bc[...]
     copies = []
     for d in (1, 2, 3):
         for half in (0, 1):
             place, device = ph.along(half, True, d)
             copies.append(ph.send(s1.at[half, :, rows_of(place, 32), :], bx.at[half, d - 1], device))
-    if beside is not None:
-        beside()
+    beside()
     for copy in copies:
         copy.wait_recv()
     for half in (0, 1):
@@ -279,11 +282,12 @@
     for d in (1, 2, 3):
         copies.append(ph.send(s3, spread.at[d], {"snap": ph.other(d)}))
     spread[0] = s3[...]
+    after()
     for copy in copies:
         copy.wait_recv()
 
 
-def give_over_space(ph, chunk, g1, g2, out, beside=None):
+def give_over_space(ph, chunk, g1, out, beside=None):
     copies = []
     for half in (0, 1):
         mine = rows_of(ph.own(half, False), 8)
@@ -293,23 +297,27 @@
         g1[half, :, mine, :] = chunk[half]
     for copy in copies:
         copy.wait_recv()
-    copies = []
+    twin = {"space": ph.space(ph.x, ph.y, 1 - ph.core)}
+    copies, last = {}, []
+    for d in (1, 3, 2):
+        for half in (0, 1):
+            mine = rows_of(ph.core * 4 + ph.own(half, True), 32)
+            _, device = ph.along(half, True, d)
+            copies[d, half] = ph.send(g1.at[half], out.at[half, :, mine, :], device)
     for half in (0, 1):
-        mine = rows_of(ph.own(half, True), 32)
-        for d in (1, 2, 3):
-            _, device = ph.along(half, True, d)
-            copies.append(ph.send(g1.at[half], g2.at[half, :, mine, :], device))
-        g2[half, :, mine, :] = g1[half]
+        mine = rows_of(ph.core * 4 + ph.own(half, True), 32)
+        last.append(ph.send(g1.at[half], out.at[half, :, mine, :], twin))
+        out[half, :, mine, :] = g1[half]
     if beside is not None:
         beside()
-    for copy in copies:
+    for d in (1, 3, 2):
+        for half in (0, 1):
+            copies[d, half].wait_recv()
+            origin = lax.rem(ph.own(half, True) + 4 - d, 4)
+            theirs = out.at[half, :, rows_of(ph.core * 4 + origin, 32), :]
+            last.append(ph.send(theirs, theirs, twin))
+    for copy in last:
         copy.wait_recv()
-    mine = rows_of(ph.core, 128)
-    copy = ph.send(
-        g2, out.at[:, :, mine, :], {"space": ph.space(ph.x, ph.y, 1 - ph.core)}
-    )
-    out[:, :, mine, :] = g2[...]
-    copy.wait_recv()
 
 
 def put_halves(ref, index, square):
@@ -327,19 +335,22 @@
 
 def first_sum(
     count_ref, x_ref, volume_ref, om_ref, out_ref, parts_ref, zo_ref, weight_ref,
-    part, bc, bx, by, s1, s2, s3, spread, chunk, g1, g2, got, sends, arrivals,
-    raw, om_local, loads, local, parts, m, zo, wide
+    part, bc, bx, by, s1, s2, s3, spread, chunk, g1, got, sends, arrivals,
+    raw, om_local, volume_local, loads, local, parts, m, zo, wide
 ):
     ph = Phases(sends, arrivals)
     load = pltpu.make_async_copy(x_ref, raw, loads.at[0])
     load.start()
     om_load = pltpu.make_async_copy(om_ref.at[ph.core], om_local, loads.at[1])
     om_load.start()
+    volume_load = pltpu.make_async_copy(volume_ref, volume_local, loads.at[2])
+    volume_load.start()
     ph.greet(ph.peers())
     used = count_ref[0] * BLOCK
     rows = raw.shape[0]
     total = rows * lax.axis_size("space")
-    volume = volume_ref[...].reshape(1, rows)
+    volume_load.wait()
+    volume = volume_local[...].reshape(1, rows)
     weight = jnp.where(iota((1, rows), 1) < used, volume, 0.0) / total
     weight_ref[...] = weight
     load.wait()
@@ -360,12 +371,14 @@
     m[...] = mm(om, om, TN)
     mine = zo.at[ph.core]
     sum_over_space(
-        ph, part, bc, bx, by, s1, s2, s3, spread, lambda: chol_upper(m, mine, wide)
+        ph, part, bc, bx, by, s1, s2, s3, spread,
+        [lambda: None],
+        lambda: chol_upper(m, mine, wide),
+        lambda: bulk.append(give_rows(3)),
     )
-    bulk.append(give_rows(3))
     for d in range(4):
         chunk[:, d] = spread[d, :, 0]
-    give_over_space(ph, chunk, g1, g2, got, lambda: chol_lower(mine, wide))
+    give_over_space(ph, chunk, g1, got, lambda: chol_lower(mine, wide))
     factor_copy = ph.send(mine, mine, {"space": ph.space(ph.x, ph.y, 1 - ph.core)})
     for d in range(4):
         out_ref[d] = whole(got, d)
@@ -393,7 +406,7 @@
 
 def second_sum(
     z_ref, x_ref, weight_ref, om_ref, zo_ref, out_ref, sk_ref, q_ref,
-    part, bc, bx, by, s1, s2, s3, spread, chunk, g1, g2, got, sends, arrivals, base, sketch
+    part, bc, bx, by, s1, s2, s3, spread, chunk, g1, got, sends, arrivals, base, sketch
 ):
     ph = Phases(sends, arrivals)
     ph.greet(ph.peers())
@@ -407,9 +420,15 @@
         low, high = base[2 * pair], base[2 * pair + 1]
         both = mm(low, om_ref[0, :rank, :]) + mm(high, om_ref[0, rank:, :])
         mine[:, pair * rank : (pair + 1) * rank] = both.astype(BF16)
-        put_halves(part, pair, mm2(jnp.transpose(low).astype(F32) * weight, high))
-    low, high = mine[:, :rank], mine[:, rank:]
-    put_halves(part, 2, mm2(jnp.transpose(low).astype(F32) * weight, high))
+
+    def cross_gram(index, low, high):
+        put_halves(part, index, mm2(jnp.transpose(low).astype(F32) * weight, high))
+
+    makers = [
+        lambda: cross_gram(0, base[0], base[1]),
+        lambda: cross_gram(1, base[2], base[3]),
+        lambda: cross_gram(2, mine[:, :rank], mine[:, rank:]),
+    ]
     ph.met(10)
     piece = quarter // 2
 
@@ -423,10 +442,14 @@
             q_ref[level, 1] = mm2r(om_ref[level, rank:, :], zo_ref[level], NT)
 
     bulk = [give_sketch(2, 0), give_sketch(1, 0)]
-    sum_over_space(ph, part, bc, bx, by, s1, s2, s3, spread, omega_products)
-    bulk += [give_sketch(2, 1), give_sketch(1, 1)]
+    sum_over_space(
+        ph, part, bc, bx, by, s1, s2, s3, spread,
+        makers,
+        omega_products,
+        lambda: bulk.extend([give_sketch(2, 1), give_sketch(1, 1)]),
+    )
     chunk[...] = (spread[0] + spread[1]) + (spread[2] + spread[3])
-    give_over_space(ph, chunk, g1, g2, got)
+    give_over_space(ph, chunk, g1, got)
     for d in range(3):
         out_ref[d] = whole(got, d)
     for copy in bulk:
@@ -437,7 +460,7 @@
     ph.finish()
 
 
-def sum_scratch(before, after, copies=29):
+def sum_scratch(before, after, copies):
     return [
         pltpu.VMEM((2, before, 128, 128), F32),
         pltpu.VMEM((2, 3, before, 32, 128), F32),
@@ -448,7 +471,6 @@
         pltpu.VMEM((4, 2, before, 8, 128), F32),
         pltpu.VMEM((2, after, 8, 128), F32),
         pltpu.VMEM((2, after, 32, 128), F32),
-        pltpu.VMEM((2, after, 128, 128), F32),
         pltpu.VMEM((2, after, 256, 128), F32),
         pltpu.SemaphoreType.DMA((copies,)),
         pltpu.SemaphoreType.DMA((copies,)),
@@ -478,7 +500,7 @@
 
 
 def spread_kernel(
-    rim_ref, sk_ref, mix_ref, base_ref, rims_ref, own, base, rim_out, rim_in, sends, arrivals
+    rim_ref, sk_ref, mix_ref, out_ref, own, base, rim_out, rim_in, sends, arrivals
 ):
     ph = Phases(sends, arrivals)
     me, n = lax.axis_index("space"), lax.axis_size("space")
@@ -521,46 +543,55 @@
     base[pl.ds((1 - upper) * half + second * quarter, quarter)] = rows_from(sk_ref[2])
     for swap in swaps:
         swap.wait_recv()
-    rims_ref[:BLOCK, :] = jnp.where(me > 0, rim_in[0, 0] + rim_in[0, 1], 0)
-    rims_ref[BLOCK:, :] = jnp.where(me < n - 1, rim_in[1, 0] + rim_in[1, 1], 0)
+    blocks = base.shape[0]
+    out_ref[blocks] = jnp.where(me > 0, rim_in[0, 0] + rim_in[0, 1], 0)
+    out_ref[blocks + 1] = jnp.where(me < n - 1, rim_in[1, 0] + rim_in[1, 1], 0)
     copy.wait_recv()
-    base_ref[...] = base[...].reshape(base_ref.shape)
+    out_ref[:blocks] = base[...]
     ph.finish()
 
 
-def product_kernel(cols_ref, count_ref, full_ref, rims_ref, jac_ref, base_ref, out_ref, held):
-    rows, rank = full_ref.shape
-    blocks = rows // BLOCK
-    base_ref[...] = full_ref[...]
-    held[:rows, :] = full_ref[...]
-    held[rows:, :] = rims_ref[...]
+def product_kernel(cols_ref, count_ref, full_ref, jac_ref, base_ref, out_ref, product, sems):
+    rank = full_ref.shape[2]
+    blocks = jac_ref.shape[0] // BLOCK
     count = count_ref[0]
-
-    def block(b, _):
-        here = pl.ds(pl.multiple_of(b * BLOCK, BLOCK), BLOCK)
-        picked = [
-            held[pl.ds(pl.multiple_of(cols_ref[b, k] * BLOCK, BLOCK), BLOCK), :] for k in range(NNZ)
-        ]
-        product = mm(jac_ref[here, :], jnp.concatenate(picked, axis=0))
-        out_ref[here, :] = jnp.where(b < count, product, 0.0).astype(BF16)
-        return 0
-
-    lax.fori_loop(0, blocks, block, 0, unroll=2)
+    copies = [pltpu.make_async_copy(full_ref.at[pl.ds(0, blocks)], base_ref, sems.at[0])]
+    copies[0].start()
+    pieces = 4
+    size = blocks // pieces
+    for piece in range(pieces):
+
+        def block(i, _):
+            b = piece * size + i
+            picked = [full_ref[cols_ref[b, k]] for k in range(NNZ)]
+            here = pl.ds(pl.multiple_of(b * BLOCK, BLOCK), BLOCK)
+            found = mm(jac_ref[here, :], jnp.concatenate(picked, axis=0))
+            product[b] = jnp.where(b < count, found, 0.0).astype(BF16)
+            return 0
+
+        lax.fori_loop(0, size, block, 0, unroll=3)
+        done = pl.ds(piece * size, size)
+        copies.append(
+            pltpu.make_async_copy(product.at[done], out_ref.at[done], sems.at[piece + 1])
+        )
+        copies[-1].start()
+    for copy in copies:
+        copy.wait()
 
 
 VM = pl.BlockSpec(memory_space=pltpu.VMEM)
 SM = pl.BlockSpec(memory_space=pltpu.SMEM)
-ANY = pl.BlockSpec(memory_space=pl.ANY)
-
-
-def call(body, outs, ins, scratch, name, **params):
+HBM = pl.BlockSpec(memory_space=pltpu.HBM)
+
+
+def call(body, outs, ins, scratch, name, out=VM, limit=VMEM_LIMIT, **params):
     return pl.pallas_call(
         body,
         out_shape=outs,
         in_specs=ins,
-        out_specs=jax.tree.map(lambda _: VM, outs),
+        out_specs=jax.tree.map(lambda _: out, outs),
         scratch_shapes=scratch,
-        compiler_params=pltpu.CompilerParams(vmem_limit_bytes=VMEM_LIMIT, **params),
+        compiler_params=pltpu.CompilerParams(vmem_limit_bytes=limit, **params),
         name=name,
     )
 
@@ -582,13 +613,14 @@
             jax.ShapeDtypeStruct((2, rank, rank), F32),
             jax.ShapeDtypeStruct((1, rows), F32),
         ],
-        [SM, ANY, VM, ANY],
+        [SM, HBM, HBM, HBM],
         [pltpu.VMEM((2, 1, rank, rank // 2), F32)]
-        + sum_scratch(1, 4, 33)
+        + sum_scratch(1, 4, 40)
         + [
             pltpu.VMEM((rows, rank), BF16),
             pltpu.VMEM((2 * rank, rank), BF16),
-            pltpu.SemaphoreType.DMA((2,)),
+            pltpu.VMEM((rows,), F32),
+            pltpu.SemaphoreType.DMA((3,)),
             pltpu.VMEM((rows, rank), BF16),
             pltpu.VMEM((3, quarter, rank), BF16),
             pltpu.VMEM(square, F32),
@@ -596,6 +628,7 @@
             wide,
         ],
         "first_sum",
+        limit=60 * 1024 * 1024,
         collective_id=0,
         has_side_effects=True,
     )(counts, snapshots, cell_volume, omega)
@@ -615,7 +648,7 @@
         ],
         [VM] * 5,
         [pltpu.VMEM((2, 3, rank, rank // 2), F32)]
-        + sum_scratch(3, 3, 33)
+        + sum_scratch(3, 3, 42)
         + [pltpu.VMEM((4, quarter, rank), BF16), pltpu.VMEM((4, quarter, 2 * rank), BF16)],
         "second_sum",
         collective_id=1,
@@ -628,12 +661,9 @@
         [squares(3), squares(3), squares(2), squares(2), squares(2), wide],
         "merge_factors",
     )(cross, omega, starts, products)
-    full, rims = call(
+    full = call(
         spread_kernel,
-        [
-            jax.ShapeDtypeStruct((rows, rank), BF16),
-            jax.ShapeDtypeStruct((2 * BLOCK, rank), BF16),
-        ],
+        jax.ShapeDtypeStruct((blocks + 2, BLOCK, rank), BF16),
         [SM, VM, VM],
         [
             pltpu.VMEM((blocks // 2, BLOCK, rank), BF16),
@@ -649,12 +679,13 @@
     )(rim_rows, sketch, mix)
     basis, product = call(
         product_kernel,
-        [jax.ShapeDtypeStruct((rows, rank), BF16)] * 2,
-        [SM, SM, VM, VM, VM],
-        [pltpu.VMEM((rows + 2 * BLOCK, rank), BF16)],
+        [jax.ShapeDtypeStruct((blocks, BLOCK, rank), BF16)] * 2,
+        [SM, SM, VM, VM],
+        [pltpu.VMEM((blocks, BLOCK, rank), BF16), pltpu.SemaphoreType.DMA((5,))],
         "jac_product",
-    )(jac_cols, counts, full, rims, jacobian)
-    return (basis, product)
+        out=HBM,
+    )(jac_cols, counts, full, jacobian)
+    return (basis.reshape(rows, rank), product.reshape(rows, rank))
 
 
 def solution(mesh):

time: 141 us -> 146 us (1.035)
  the two profiles are of different devices: /device:TPU:128 before, /device:TPU:288 now
where the time goes in v5:
time: 146 us
  Pallas kernels  143 us (98%)
  between operations  1.57 us (1%)
    pallas_call x1, Pallas kernels, on_device(): call(gram_factors, jax.ShapeDtypeStruct((4, rank, rank), F32), [VM], [squ...  52.2 us
    pallas_call x1, Pallas kernels, on_device(): call(first_sum, [jax.ShapeDtypeStruct((4, rank, rank), F32), jax.ShapeDty...  35.6 us
    pallas_call x1, Pallas kernels, on_device(): call(second_sum, [jax.ShapeDtypeStruct((3, rank, rank), F32), jax.ShapeDt...  31.4 us
    pallas_call x1, Pallas kernels, on_device(): call(spread_kernel, jax.ShapeDtypeStruct((blocks + 2, BLOCK, rank), BF16)...  13.2 us
    pallas_call x1, Pallas kernels, on_device(): call(merge_factors, jax.ShapeDtypeStruct((2 * rank, rank), F32), [VM] * 4...  6.53 us
    pallas_call x1, Pallas kernels, on_device(): call(product_kernel, [jax.ShapeDtypeStruct((blocks, BLOCK, rank), BF16)]...  3.58 us

profile of v5, /device:TPU:288, one launch (start us, length us, event | category | flops | bytes accessed | tf_op | source)
XLA Modules:
  0.0 145.5 jit_solution(1343342332563027602)
XLA Ops:
  1.3 0.0 copy-start
  1.3 35.6 %first_sum.1 = (f32[4,256,256]{2,1,0:T(8,128)}, bf16[4,384,256]{2,1,0:T(8,128)(2,1)}, f32[2,256,256]{2,1,0:T(8,128)}, f32[1,1536]{1,0:T(1,128)}) custom-call(s32[1]{0:T(128)S(6)} %copy.10.count_ref, bf16[1536,256]{1,0:T(8,128)(2,1)} %x_ref.1, f32[1536]{0:T(1024)} %volume_ref.1, bf16[2,512,256]{2,1,0:T(8,128)(2,1)} %om_ref.5), custom_call_target="tpu_custom_call" | custom-call | tf_op jit(solution)/shard_map/first_sum/pallas_call | solution.py:608
  36.9 0.0 copy-start.1
  36.9 0.0 copy-start.3
  36.9 1.3 copy-done.3
  38.2 0.0 copy-start.4
  38.2 0.0 copy-start.5
  38.2 52.2 %gram_factors.1.z_ref = f32[4,256,256]{2,1,0:T(8,128)S(1)} custom-call(f32[4,256,256]{2,1,0:T(8,128)S(1)} %copy-done.3), custom_call_target="tpu_custom_call" | custom-call | tf_op jit(solution)/shard_map/gram_factors/pallas_call | solution.py:635
  90.5 0.0 copy-done
  90.5 0.0 copy-done.1
  90.5 0.0 copy-done.4
  90.5 0.0 copy-done.5
  90.5 31.4 %second_sum.1 = (f32[3,256,256]{2,1,0:T(8,128)S(1)}, bf16[3,384,512]{2,1,0:T(8,128)(2,1)S(1)}, f32[2,2,256,256]{3,2,1,0:T(8,128)S(1)}) custom-call(f32[4,256,256]{2,1,0:T(8,128)S(1)} %gram_factors.1.z_ref, bf16[4,384,256]{2,1,0:T(8,128)(2,1)S(1)} %copy-done.4, f32[1,1536]{1,0:T(1,128)S(1)} %copy-done.5, bf16[2,512,256]{2,1,0:T(8,128)(2,1)S(1)} %copy-done, ...), custom_call_target="tpu_custom_call" | custom-call | tf_op jit(solution)/shard_map/second_sum/pallas_call | solution.py:642
  121.9 0.0 copy-start.6
  121.9 6.5 %merge_factors.1.mix_ref = f32[512,256]{1,0:T(8,128)S(1)} custom-call(f32[3,256,256]{2,1,0:T(8,128)S(1)} %get-tuple-element.16.c_ref, bf16[2,512,256]{2,1,0:T(8,128)(2,1)S(1)} %copy-done, f32[2,256,256]{2,1,0:T(8,128)S(1)} %copy-done.1, f32[2,2,256,256]{3,2,1,0:T(8,128)S(1)} %get-tuple-element.17.q_ref), custom_call_target="tpu_custom_call" | custom-call | tf_op jit(solution)/shard_map/merge_factors/pallas_call | solution.py:657
  128.5 0.0 copy-start.7
  128.5 0.0 copy-start.2
  128.5 0.0 copy-done.6
  128.5 13.2 %spread_rows.1.full_ref = bf16[26,64,256]{2,1,0:T(8,128)(2,1)S(1)} custom-call(s32[1,2]{1,0:T(1,128)S(1)} %copy-done.6, bf16[3,384,512]{2,1,0:T(8,128)(2,1)S(1)} %get-tuple-element.15.sk_ref, f32[512,256]{1,0:T(8,128)S(1)} %merge_factors.1.mix_ref), custom_call_target="tpu_custom_call" | custom-call | tf_op jit(solution)/shard_map/spread_rows/pallas_call | solution.py:664
  141.7 0.0 copy-done.7
  141.7 0.1 copy.9.cols_ref
  141.8 0.0 copy-done.2
  141.8 3.6 %jac_product.1 = (bf16[24,64,256]{2,1,0:T(8,128)(2,1)}, bf16[24,64,256]{2,1,0:T(8,128)(2,1)}) custom-call(s32[24,8]{1,0:T(8,128)S(1)} %copy.9.cols_ref, s32[1]{0:T(128)S(6)} %copy.10.count_ref, bf16[26,64,256]{2,1,0:T(8,128)(2,1)S(1)} %spread_rows.1.full_ref, bf16[1536,512]{1,0:T(8,128)(2,1)S(1)} %copy-done.2), custom_call_target="tpu_custom_call" | custom-call | tf_op jit(solution)/shard_map/jac_product/pallas_call | solution.py:680
Async XLA Ops:
  1.3 89.2 %copy-start = (bf16[2,512,256]{2,1,0:T(8,128)(2,1)S(1)}, bf16[2,512,256]{2,1,0:T(8,128)(2,1)}, u32[]{:S(2)}) copy-start(bf16[2,512,256]{2,1,0:T(8,128)(2,1)} %om_ref.5) | copy-start | bytes 1572868
  36.9 53.5 %copy-start.1 = (f32[2,256,256]{2,1,0:T(8,128)S(1)}, f32[2,256,256]{2,1,0:T(8,128)}, u32[]{:S(2)}) copy-start(f32[2,256,256]{2,1,0:T(8,128)} %get-tuple-element.14.zo_ref) | copy-start | bytes 1572868
  36.9 1.3 copy-start.3
  38.2 52.3 %copy-start.4 = (bf16[4,384,256]{2,1,0:T(8,128)(2,1)S(1)}, bf16[4,384,256]{2,1,0:T(8,128)(2,1)}, u32[]{:S(2)}) copy-start(bf16[4,384,256]{2,1,0:T(8,128)(2,1)} %get-tuple-element.12.x_ref) | copy-start | bytes 2359300
  38.2 52.3 %copy-start.5 = (f32[1,1536]{1,0:T(1,128)S(1)}, f32[1,1536]{1,0:T(1,128)}, u32[]{:S(2)}) copy-start(f32[1,1536]{1,0:T(1,128)} %get-tuple-element.13.weight_ref) | copy-start | bytes 18436
  121.9 6.6 %copy-start.6 = (s32[1,2]{1,0:T(1,128)S(1)}, s32[1,2]{1,0:T(1,128)}, u32[]{:S(2)}) copy-start(s32[1,2]{1,0:T(1,128)} %rim_ref.1) | copy-start | bytes 28
  128.5 13.2 %copy-start.7 = (s32[24,8]{0,1:T(8,128)S(1)}, s32[24,8]{0,1:T(8,128)}, u32[]{:S(2)}) copy-start(s32[24,8]{0,1:T(8,128)} %param.11) | copy-start | bytes 2308
  128.5 13.3 %copy-start.2 = (bf16[1536,512]{1,0:T(8,128)(2,1)S(1)}, bf16[1536,512]{1,0:T(8,128)(2,1)}, u32[]{:S(2)}) copy-start(bf16[1536,512]{1,0:T(8,128)(2,1)} %jac_ref.1) | copy-start | bytes 4718596

commit v6 on v5

--- a/solution.py
+++ b/solution.py
@@ -282,9 +282,9 @@
     for d in (1, 2, 3):
         copies.append(ph.send(s3, spread.at[d], {"snap": ph.other(d)}))
     spread[0] = s3[...]
-    after()
     for copy in copies:
         copy.wait_recv()
+    after()
 
 
 def give_over_space(ph, chunk, g1, out, beside=None):
@@ -482,8 +482,7 @@
     a[...] = eye(cross.shape[0]) + t[...] + jnp.transpose(t[...])
 
 
-def merge_factors(c_ref, om_ref, zo_ref, q_ref, out_ref, a, z, first, start, t, wide):
-    rank = om_ref.shape[2]
+def merge_factors(c_ref, zo_ref, q_ref, z, a, first, start, t, wide):
     for pair in (0, 1):
         near_identity(q_ref[0, 0], c_ref[pair], q_ref[0, 1], a.at[pair], t.at[pair])
         z[pair] = zo_ref[0]
@@ -493,14 +492,10 @@
     near_identity(t[0], c_ref[2], t[1], a.at[2], t.at[0])
     z[2] = zo_ref[1]
     factor(a.at[pl.ds(2, 1)], z.at[pl.ds(2, 1)], first, start, wide, 1, 3, 8)
-    last = z[2]
-    for pair in (0, 1):
-        u = mm2r(om_ref[1, pair * rank : (pair + 1) * rank, :], last, NT)
-        out_ref[pair * rank : (pair + 1) * rank, :] = mm3(jnp.transpose(z[pair]), u)
 
 
 def spread_kernel(
-    rim_ref, sk_ref, mix_ref, out_ref, own, base, rim_out, rim_in, sends, arrivals
+    rim_ref, sk_ref, z_ref, om_ref, out_ref, own, base, rim_out, rim_in, sends, arrivals
 ):
     ph = Phases(sends, arrivals)
     me, n = lax.axis_index("space"), lax.axis_size("space")
@@ -509,7 +504,12 @@
     targets = [{"space": before}, {"space": after}]
     targets += [{"space": before, "snap": near}, {"space": after, "snap": near}]
     ph.greet([{"snap": near}] + targets)
-    high, low = split(mix_ref[...])
+    rank = om_ref.shape[2]
+    mix = []
+    for pair in (0, 1):
+        u = mm2r(om_ref[1, pair * rank : (pair + 1) * rank, :], z_ref[2], NT)
+        mix.append(mm3(jnp.transpose(z_ref[pair]), u))
+    high, low = split(jnp.concatenate(mix, axis=0))
     half = base.shape[0] // 2
     quarter = half // 2
     upper = lax.rem(ph.place, 2)
@@ -654,17 +654,17 @@
         collective_id=1,
         has_side_effects=True,
     )(factors, parts, weight, omega, starts)
-    mix = call(
+    merged = call(
         merge_factors,
-        jax.ShapeDtypeStruct((2 * rank, rank), F32),
-        [VM] * 4,
-        [squares(3), squares(3), squares(2), squares(2), squares(2), wide],
+        jax.ShapeDtypeStruct((3, rank, rank), F32),
+        [VM] * 3,
+        [squares(3), squares(2), squares(2), squares(2), wide],
         "merge_factors",
-    )(cross, omega, starts, products)
+    )(cross, starts, products)
     full = call(
         spread_kernel,
         jax.ShapeDtypeStruct((blocks + 2, BLOCK, rank), BF16),
-        [SM, VM, VM],
+        [SM, VM, VM, VM],
         [
             pltpu.VMEM((blocks // 2, BLOCK, rank), BF16),
             pltpu.VMEM((blocks, BLOCK, rank), BF16),
@@ -676,7 +676,7 @@
         "spread_rows",
         collective_id=2,
         has_side_effects=True,
-    )(rim_rows, sketch, mix)
+    )(rim_rows, sketch, merged, omega)
     basis, product = call(
         product_kernel,
         [jax.ShapeDtypeStruct((blocks, BLOCK, rank), BF16)] * 2,

time: 146 us -> 140 us (0.959)
  the two profiles are of different devices: /device:TPU:288 before, /device:TPU:128 now
where the time goes in v6:
time: 140 us
  Pallas kernels  137 us (98%)
  between operations  1.57 us (1%)
    pallas_call x1, Pallas kernels, on_device(): call(gram_factors, jax.ShapeDtypeStruct((4, rank, rank), F32), [VM], [squ...  52.2 us
    pallas_call x1, Pallas kernels, on_device(): call(first_sum, [jax.ShapeDtypeStruct((4, rank, rank), F32), jax.ShapeDty...  34.7 us
    pallas_call x1, Pallas kernels, on_device(): call(second_sum, [jax.ShapeDtypeStruct((3, rank, rank), F32), jax.ShapeDt...  27.7 us
    pallas_call x1, Pallas kernels, on_device(): call(spread_kernel, jax.ShapeDtypeStruct((blocks + 2, BLOCK, rank), BF16)...  13.3 us
    pallas_call x1, Pallas kernels, on_device(): call(merge_factors, jax.ShapeDtypeStruct((3, rank, rank), F32), [VM] * 3,...  5.77 us
    pallas_call x1, Pallas kernels, on_device(): call(product_kernel, [jax.ShapeDtypeStruct((blocks, BLOCK, rank), BF16)]...  3.58 us

profile of v6, /device:TPU:128, one launch (start us, length us, event | category | flops | bytes accessed | tf_op | source)
XLA Modules:
  0.0 140.2 jit_solution(588426597820123196)
XLA Ops:
  1.3 0.0 copy-start
  1.3 34.7 %first_sum.1 = (f32[4,256,256]{2,1,0:T(8,128)}, bf16[4,384,256]{2,1,0:T(8,128)(2,1)}, f32[2,256,256]{2,1,0:T(8,128)}, f32[1,1536]{1,0:T(1,128)}) custom-call(s32[1]{0:T(128)S(6)} %copy.10.count_ref, bf16[1536,256]{1,0:T(8,128)(2,1)} %x_ref.1, f32[1536]{0:T(1024)} %volume_ref.1, bf16[2,512,256]{2,1,0:T(8,128)(2,1)} %om_ref.5), custom_call_target="tpu_custom_call" | custom-call | tf_op jit(solution)/shard_map/first_sum/pallas_call | solution.py:608
  36.0 0.0 copy-start.1
  36.0 0.0 copy-start.3
  36.0 1.3 copy-done.3
  37.3 0.0 copy-start.4
  37.3 0.0 copy-start.5
  37.3 52.2 %gram_factors.1.z_ref = f32[4,256,256]{2,1,0:T(8,128)S(1)} custom-call(f32[4,256,256]{2,1,0:T(8,128)S(1)} %copy-done.3), custom_call_target="tpu_custom_call" | custom-call | tf_op jit(solution)/shard_map/gram_factors/pallas_call | solution.py:635
  89.5 0.0 copy-done
  89.5 0.0 copy-done.1
  89.5 0.0 copy-done.4
  89.5 0.0 copy-done.5
  89.5 27.7 %second_sum.1 = (f32[3,256,256]{2,1,0:T(8,128)S(1)}, bf16[3,384,512]{2,1,0:T(8,128)(2,1)S(1)}, f32[2,2,256,256]{3,2,1,0:T(8,128)S(1)}) custom-call(f32[4,256,256]{2,1,0:T(8,128)S(1)} %gram_factors.1.z_ref, bf16[4,384,256]{2,1,0:T(8,128)(2,1)S(1)} %copy-done.4, f32[1,1536]{1,0:T(1,128)S(1)} %copy-done.5, bf16[2,512,256]{2,1,0:T(8,128)(2,1)S(1)} %copy-done, ...), custom_call_target="tpu_custom_call" | custom-call | tf_op jit(solution)/shard_map/second_sum/pallas_call | solution.py:642
  117.3 0.0 copy-start.6
  117.3 5.8 %merge_factors.1.z_ref = f32[3,256,256]{2,1,0:T(8,128)S(1)} custom-call(f32[3,256,256]{2,1,0:T(8,128)S(1)} %get-tuple-element.16.c_ref, f32[2,256,256]{2,1,0:T(8,128)S(1)} %copy-done.1, f32[2,2,256,256]{3,2,1,0:T(8,128)S(1)} %get-tuple-element.17.q_ref), custom_call_target="tpu_custom_call" | custom-call | tf_op jit(solution)/shard_map/merge_factors/pallas_call | solution.py:657
  123.1 0.0 copy-done.6
  123.1 0.0 copy-start.7
  123.1 0.0 copy-start.2
  123.1 13.3 %spread_rows.1.full_ref = bf16[26,64,256]{2,1,0:T(8,128)(2,1)S(1)} custom-call(s32[1,2]{1,0:T(1,128)S(1)} %copy-done.6, bf16[3,384,512]{2,1,0:T(8,128)(2,1)S(1)} %get-tuple-element.15.sk_ref, f32[3,256,256]{2,1,0:T(8,128)S(1)} %merge_factors.1.z_ref, bf16[2,512,256]{2,1,0:T(8,128)(2,1)S(1)} %copy-done), custom_call_target="tpu_custom_call" | custom-call | tf_op jit(solution)/shard_map/spread_rows/pallas_call | solution.py:664
  136.4 0.0 copy-done.7
  136.4 0.1 copy.9.cols_ref
  136.5 0.0 copy-done.2
  136.5 3.6 %jac_product.1 = (bf16[24,64,256]{2,1,0:T(8,128)(2,1)}, bf16[24,64,256]{2,1,0:T(8,128)(2,1)}) custom-call(s32[24,8]{1,0:T(8,128)S(1)} %copy.9.cols_ref, s32[1]{0:T(128)S(6)} %copy.10.count_ref, bf16[26,64,256]{2,1,0:T(8,128)(2,1)S(1)} %spread_rows.1.full_ref, bf16[1536,512]{1,0:T(8,128)(2,1)S(1)} %copy-done.2), custom_call_target="tpu_custom_call" | custom-call | tf_op jit(solution)/shard_map/jac_product/pallas_call | solution.py:680
Async XLA Ops:
  1.3 88.2 %copy-start = (bf16[2,512,256]{2,1,0:T(8,128)(2,1)S(1)}, bf16[2,512,256]{2,1,0:T(8,128)(2,1)}, u32[]{:S(2)}) copy-start(bf16[2,512,256]{2,1,0:T(8,128)(2,1)} %om_ref.5) | copy-start | bytes 1572868
  36.0 53.5 %copy-start.1 = (f32[2,256,256]{2,1,0:T(8,128)S(1)}, f32[2,256,256]{2,1,0:T(8,128)}, u32[]{:S(2)}) copy-start(f32[2,256,256]{2,1,0:T(8,128)} %get-tuple-element.14.zo_ref) | copy-start | bytes 1572868
  36.0 1.3 copy-start.3
  37.3 52.3 %copy-start.4 = (bf16[4,384,256]{2,1,0:T(8,128)(2,1)S(1)}, bf16[4,384,256]{2,1,0:T(8,128)(2,1)}, u32[]{:S(2)}) copy-start(bf16[4,384,256]{2,1,0:T(8,128)(2,1)} %get-tuple-element.12.x_ref) | copy-start | bytes 2359300
  37.3 52.3 %copy-start.5 = (f32[1,1536]{1,0:T(1,128)S(1)}, f32[1,1536]{1,0:T(1,128)}, u32[]{:S(2)}) copy-start(f32[1,1536]{1,0:T(1,128)} %get-tuple-element.13.weight_ref) | copy-start | bytes 18436
  117.3 5.8 %copy-start.6 = (s32[1,2]{1,0:T(1,128)S(1)}, s32[1,2]{1,0:T(1,128)}, u32[]{:S(2)}) copy-start(s32[1,2]{1,0:T(1,128)} %rim_ref.1) | copy-start | bytes 28
  123.1 13.3 %copy-start.7 = (s32[24,8]{0,1:T(8,128)S(1)}, s32[24,8]{0,1:T(8,128)}, u32[]{:S(2)}) copy-start(s32[24,8]{0,1:T(8,128)} %param.11) | copy-start | bytes 2308
  123.1 13.4 %copy-start.2 = (bf16[1536,512]{1,0:T(8,128)(2,1)S(1)}, bf16[1536,512]{1,0:T(8,128)(2,1)}, u32[]{:S(2)}) copy-start(bf16[1536,512]{1,0:T(8,128)(2,1)} %jac_ref.1) | copy-start | bytes 4718596

commit v7 on v6

--- a/solution.py
+++ b/solution.py
@@ -245,17 +245,10 @@
     return pl.ds(pl.multiple_of(place * size, size), size)
 
 
-def sum_over_space(ph, part, bc, bx, by, s1, s2, s3, spread, makers, beside, after):
+def sum_over_space(ph, part, bc, bx, by, s1, s2, s3, spread, beside, after):
     twin = {"space": ph.space(ph.x, ph.y, 1 - ph.core)}
-    copies = []
-    for i, make in enumerate(makers):
-        make()
-        which = pl.ds(i, 1)
-        copies.append(
-            ph.send(part.at[:, which, rows_of(1 - ph.core, 128), :], bc.at[:, which], twin)
-        )
-    for copy in copies:
-        copy.wait_recv()
+    copy = ph.send(part.at[:, :, rows_of(1 - ph.core, 128), :], bc, twin)
+    copy.wait_recv()
     s1[...] = part[:, :, rows_of(ph.core, 128), :] + bc[...]
     copies = []
     for d in (1, 2, 3):
@@ -372,7 +365,6 @@
     mine = zo.at[ph.core]
     sum_over_space(
         ph, part, bc, bx, by, s1, s2, s3, spread,
-        [lambda: None],
         lambda: chol_upper(m, mine, wide),
         lambda: bulk.append(give_rows(3)),
     )
@@ -421,14 +413,9 @@
         both = mm(low, om_ref[0, :rank, :]) + mm(high, om_ref[0, rank:, :])
         mine[:, pair * rank : (pair + 1) * rank] = both.astype(BF16)
 
-    def cross_gram(index, low, high):
+    pairs = ((base[0], base[1]), (base[2], base[3]), (mine[:, :rank], mine[:, rank:]))
+    for index, (low, high) in enumerate(pairs):
         put_halves(part, index, mm2(jnp.transpose(low).astype(F32) * weight, high))
-
-    makers = [
-        lambda: cross_gram(0, base[0], base[1]),
-        lambda: cross_gram(1, base[2], base[3]),
-        lambda: cross_gram(2, mine[:, :rank], mine[:, rank:]),
-    ]
     ph.met(10)
     piece = quarter // 2
 
@@ -444,7 +431,6 @@
     bulk = [give_sketch(2, 0), give_sketch(1, 0)]
     sum_over_space(
         ph, part, bc, bx, by, s1, s2, s3, spread,
-        makers,
         omega_products,
         lambda: bulk.extend([give_sketch(2, 1), give_sketch(1, 1)]),
     )
@@ -519,7 +505,6 @@
         found = (mm(sk, high) + mm(sk, low)).astype(BF16)
         return found.reshape(quarter, *own.shape[1:])
 
-    own[pl.ds(second * quarter, quarter)] = rows_from(sk_ref[0])
     own[pl.ds((1 - second) * quarter, quarter)] = rows_from(sk_ref[1])
     ph.met(5)
     sent = upper * half + (1 - second) * quarter
@@ -528,6 +513,7 @@
         base.at[pl.ds(sent, quarter)],
         {"snap": near},
     )
+    own[pl.ds(second * quarter, quarter)] = rows_from(sk_ref[0])
     for side in (0, 1):
         where = rim_ref[0, side] - upper * half
         block = own[jnp.clip(where, 0, half - 1)]
@@ -569,7 +555,7 @@
             product[b] = jnp.where(b < count, found, 0.0).astype(BF16)
             return 0
 
-        lax.fori_loop(0, size, block, 0, unroll=3)
+        lax.fori_loop(0, size, block, 0, unroll=6)
         done = pl.ds(piece * size, size)
         copies.append(
             pltpu.make_async_copy(product.at[done], out_ref.at[done], sems.at[piece + 1])

time: 140 us -> 139 us (level)
  Pallas kernels: 137 us -> 135 us
where the time goes in v7:
time: 139 us; the launch traced here: 138 us
  Pallas kernels  135 us (97%)
  between operations  1.59 us (1%)
    pallas_call x1, Pallas kernels, on_device(): call(gram_factors, jax.ShapeDtypeStruct((4, rank, rank), F32), [VM], [squ...  52.2 us
    pallas_call x1, Pallas kernels, on_device(): call(first_sum, [jax.ShapeDtypeStruct((4, rank, rank), F32), jax.ShapeDty...  34.7 us
    pallas_call x1, Pallas kernels, on_device(): call(second_sum, [jax.ShapeDtypeStruct((3, rank, rank), F32), jax.ShapeDt...  26.7 us
    pallas_call x1, Pallas kernels, on_device(): call(spread_kernel, jax.ShapeDtypeStruct((blocks + 2, BLOCK, rank), BF16)...  13.2 us
    pallas_call x1, Pallas kernels, on_device(): call(merge_factors, jax.ShapeDtypeStruct((3, rank, rank), F32), [VM] * 3,...  5.99 us

profile of v7, /device:TPU:128, one launch (start us, length us, event | category | flops | bytes accessed | tf_op | source)
XLA Modules:
  0.0 138.4 jit_solution(10471360522003161113)
XLA Ops:
  1.3 0.0 copy-start
  1.3 34.7 %first_sum.1 = (f32[4,256,256]{2,1,0:T(8,128)}, bf16[4,384,256]{2,1,0:T(8,128)(2,1)}, f32[2,256,256]{2,1,0:T(8,128)}, f32[1,1536]{1,0:T(1,128)}) custom-call(s32[1]{0:T(128)S(6)} %copy.10.count_ref, bf16[1536,256]{1,0:T(8,128)(2,1)} %x_ref.1, f32[1536]{0:T(1024)} %volume_ref.1, bf16[2,512,256]{2,1,0:T(8,128)(2,1)} %om_ref.5), custom_call_target="tpu_custom_call" | custom-call | tf_op jit(solution)/shard_map/first_sum/pallas_call | solution.py:594
  36.0 0.0 copy-start.1
  36.0 0.0 copy-start.3
  36.0 1.3 copy-done.3
  37.3 0.0 copy-start.4
  37.3 0.0 copy-start.5
  37.3 52.2 %gram_factors.1.z_ref = f32[4,256,256]{2,1,0:T(8,128)S(1)} custom-call(f32[4,256,256]{2,1,0:T(8,128)S(1)} %copy-done.3), custom_call_target="tpu_custom_call" | custom-call | tf_op jit(solution)/shard_map/gram_factors/pallas_call | solution.py:621
  89.5 0.0 copy-done
  89.5 0.0 copy-done.1
  89.5 0.0 copy-done.4
  89.5 0.0 copy-done.5
  89.5 26.7 %second_sum.1 = (f32[3,256,256]{2,1,0:T(8,128)S(1)}, bf16[3,384,512]{2,1,0:T(8,128)(2,1)S(1)}, f32[2,2,256,256]{3,2,1,0:T(8,128)S(1)}) custom-call(f32[4,256,256]{2,1,0:T(8,128)S(1)} %gram_factors.1.z_ref, bf16[4,384,256]{2,1,0:T(8,128)(2,1)S(1)} %copy-done.4, f32[1,1536]{1,0:T(1,128)S(1)} %copy-done.5, bf16[2,512,256]{2,1,0:T(8,128)(2,1)S(1)} %copy-done, ...), custom_call_target="tpu_custom_call" | custom-call | tf_op jit(solution)/shard_map/second_sum/pallas_call | solution.py:628
  116.2 0.0 copy-start.6
  116.2 6.0 %merge_factors.1.z_ref = f32[3,256,256]{2,1,0:T(8,128)S(1)} custom-call(f32[3,256,256]{2,1,0:T(8,128)S(1)} %get-tuple-element.16.c_ref, f32[2,256,256]{2,1,0:T(8,128)S(1)} %copy-done.1, f32[2,2,256,256]{3,2,1,0:T(8,128)S(1)} %get-tuple-element.17.q_ref), custom_call_target="tpu_custom_call" | custom-call | tf_op jit(solution)/shard_map/merge_factors/pallas_call | solution.py:643
  122.2 0.0 copy-done.6
  122.2 0.0 copy-start.7
  122.2 0.0 copy-start.2
  122.3 13.2 %spread_rows.1.full_ref = bf16[26,64,256]{2,1,0:T(8,128)(2,1)S(1)} custom-call(s32[1,2]{1,0:T(1,128)S(1)} %copy-done.6, bf16[3,384,512]{2,1,0:T(8,128)(2,1)S(1)} %get-tuple-element.15.sk_ref, f32[3,256,256]{2,1,0:T(8,128)S(1)} %merge_factors.1.z_ref, bf16[2,512,256]{2,1,0:T(8,128)(2,1)S(1)} %copy-done), custom_call_target="tpu_custom_call" | custom-call | tf_op jit(solution)/shard_map/spread_rows/pallas_call | solution.py:650
  135.5 0.0 copy-done.7
  135.5 0.1 copy.9.cols_ref
  135.6 0.0 copy-done.2
  135.6 2.7 %jac_product.1 = (bf16[24,64,256]{2,1,0:T(8,128)(2,1)}, bf16[24,64,256]{2,1,0:T(8,128)(2,1)}) custom-call(s32[24,8]{1,0:T(8,128)S(1)} %copy.9.cols_ref, s32[1]{0:T(128)S(6)} %copy.10.count_ref, bf16[26,64,256]{2,1,0:T(8,128)(2,1)S(1)} %spread_rows.1.full_ref, bf16[1536,512]{1,0:T(8,128)(2,1)S(1)} %copy-done.2), custom_call_target="tpu_custom_call" | custom-call | tf_op jit(solution)/shard_map/jac_product/pallas_call | solution.py:666
Async XLA Ops:
  1.3 88.2 %copy-start = (bf16[2,512,256]{2,1,0:T(8,128)(2,1)S(1)}, bf16[2,512,256]{2,1,0:T(8,128)(2,1)}, u32[]{:S(2)}) copy-start(bf16[2,512,256]{2,1,0:T(8,128)(2,1)} %om_ref.5) | copy-start | bytes 1572868
  36.0 53.5 %copy-start.1 = (f32[2,256,256]{2,1,0:T(8,128)S(1)}, f32[2,256,256]{2,1,0:T(8,128)}, u32[]{:S(2)}) copy-start(f32[2,256,256]{2,1,0:T(8,128)} %get-tuple-element.14.zo_ref) | copy-start | bytes 1572868
  36.0 1.3 copy-start.3
  37.3 52.3 %copy-start.4 = (bf16[4,384,256]{2,1,0:T(8,128)(2,1)S(1)}, bf16[4,384,256]{2,1,0:T(8,128)(2,1)}, u32[]{:S(2)}) copy-start(bf16[4,384,256]{2,1,0:T(8,128)(2,1)} %get-tuple-element.12.x_ref) | copy-start | bytes 2359300
  37.3 52.3 %copy-start.5 = (f32[1,1536]{1,0:T(1,128)S(1)}, f32[1,1536]{1,0:T(1,128)}, u32[]{:S(2)}) copy-start(f32[1,1536]{1,0:T(1,128)} %get-tuple-element.13.weight_ref) | copy-start | bytes 18436
  116.2 6.0 %copy-start.6 = (s32[1,2]{1,0:T(1,128)S(1)}, s32[1,2]{1,0:T(1,128)}, u32[]{:S(2)}) copy-start(s32[1,2]{1,0:T(1,128)} %rim_ref.1) | copy-start | bytes 28
  122.2 13.2 %copy-start.7 = (s32[24,8]{0,1:T(8,128)S(1)}, s32[24,8]{0,1:T(8,128)}, u32[]{:S(2)}) copy-start(s32[24,8]{0,1:T(8,128)} %param.11) | copy-start | bytes 2308
  122.2 13.3 %copy-start.2 = (bf16[1536,512]{1,0:T(8,128)(2,1)S(1)}, bf16[1536,512]{1,0:T(8,128)(2,1)}, u32[]{:S(2)}) copy-start(bf16[1536,512]{1,0:T(8,128)(2,1)} %jac_ref.1) | copy-start | bytes 4718596
